TPU v7x, 128 devices: a whole 4x4x4 slice. The times are simulated.
128 devices in a mesh: dp: 8 (over x, z_hi), mp: 16 (over z_lo, y, core).
Axes of the slice: x: 4, y: 4, z: 4 (z_hi: 2, z_lo: 2; z = z_hi * 2 + z_lo), core: 2. Of those that a mesh axis runs over, the one named last changes fastest.
Arguments:
- inputs: bfloat16 [256, 10240], P('dp', 'mp'), may hold values from -6 to 6
- out_grads: bfloat16 [256, 10240], P('dp', 'mp'), may hold values from -6 to 6
- w_in: bfloat16 [10240, 36864], P('mp', 'dp'), may hold values from -0.0625 to 0.0625
- w_out: bfloat16 [36864, 10240], P('dp', 'mp'), may hold values from -0.03125 to 0.03125
Outputs:
- in_grads: float32 [256, 10240], P('dp', 'mp')
- grad_w_in: bfloat16 [10240, 36864], P('mp', 'dp')
- grad_w_out: bfloat16 [36864, 10240], P('dp', 'mp')
All inputs are finite; a program needn't handle non-finite values.
Results may differ from a plain program's by a relative error of at most 0.005.
Values may be sent and summed in bfloat16 or wider, within the bound.
A program may use at most 128 MiB of HBM per device.

v0:
```python
import math

import jax
import jax.numpy as jnp
from jax import lax
from jax.sharding import PartitionSpec as P


def gelu_parts(preact):
    cumul = 0.5 * (1.0 + jax.scipy.special.erf(preact * (1.0 / math.sqrt(2.0))))
    density = jnp.exp(-0.5 * preact * preact) * (1.0 / math.sqrt(2.0 * math.pi))
    return (preact * cumul, cumul + preact * density)


def contract_rows(left, right):
    return lax.dot_general(
        left, right, (((0,), (0,)), ((), ())), preferred_element_type=jnp.float32
    )


def contract_cols(left, right):
    return lax.dot_general(
        left, right, (((1,), (1,)), ((), ())), preferred_element_type=jnp.float32
    )


def finish(preact, grad_act):
    gelu_value, gelu_slope = gelu_parts(preact)
    activation = gelu_value.astype(jnp.bfloat16)
    grad_preact = (grad_act * gelu_slope).astype(jnp.bfloat16)
    return (activation, grad_preact)


def local(inputs, out_grads, w_in, w_out):
    inputs_all, grads_all = (
        lax.all_gather(inputs, "dp", axis=0, tiled=True),
        lax.all_gather(out_grads, "dp", axis=0, tiled=True),
    )
    total_rows = inputs_all.shape[0]
    partial_pre = jnp.dot(inputs_all, w_in, preferred_element_type=jnp.float32)
    partial_grad = contract_cols(grads_all, w_out)
    preact, grad_act = lax.psum((partial_pre, partial_grad), "mp")
    activation, grad_preact = finish(preact, grad_act)
    factor = 1.0 / math.sqrt(total_rows)
    grad_in = (contract_rows(inputs_all, grad_preact) * factor).astype(jnp.bfloat16)
    grad_out = (contract_rows(activation, grads_all) * factor).astype(jnp.bfloat16)
    partial_all = contract_cols(grad_preact, w_in)
    in_total = lax.psum_scatter(partial_all, "dp", scatter_dimension=0, tiled=True)
    return (in_total, grad_in, grad_out)


def solution(mesh):
    return jax.shard_map(
        local,
        mesh=mesh,
        in_specs=(P("dp", "mp"), P("dp", "mp"), P("mp", "dp"), P("dp", "mp")),
        out_specs=(P("dp", "mp"), P("mp", "dp"), P("dp", "mp")),
        check_vma=False,
    )
```

profile of v0, /device:TPU:0, one launch (start us, length us, event | category | flops | bytes accessed | tf_op | source)
XLA Modules:
  0.0 325.3 jit_solution(4618956534282861747)
XLA Ops:
  7.2 0.0 all-reduce.3.cloned.1.call-start
  7.2 35.3 %all_gather.7 = bf16[256,640]{1,0:T(8,128)(2,1)S(1)} all-gather(bf16[32,640]{1,0:T(8,128)(2,1)} %param.4), channel_id=1, replica_groups=mesh['dp'=8,'mp'=16] {'dp'}, dimensions={0}, use_global_device_ids=true | all-gather | bytes 368640 | tf_op jit(solution)/shard_map/all_gather | solution.py:36
  42.5 0.0 slice-start
  42.5 35.0 %all_gather.6 = bf16[256,640]{1,0:T(8,128)(2,1)S(1)} all-gather(bf16[32,640]{1,0:T(8,128)(2,1)} %param.5), channel_id=1, replica_groups=mesh['dp'=8,'mp'=16] {'dp'}, dimensions={0}, use_global_device_ids=true | all-gather | bytes 368640 | tf_op jit(solution)/shard_map/all_gather | solution.py:37
  77.5 0.0 slice-start.1
  77.5 7.0 %fusion.7 = f32[256,4608]{1,0:T(8,128)} fusion(bf16[256,640]{1,0:T(8,128)(2,1)S(1)} %all_gather.6, bf16[4608,640]{1,0:T(8,128)(2,1)} %param.7), kind=kOutput, calls=%fused_computation.12 | convolution fusion | flops 1509949440 | bytes 10944512 | tf_op jit(solution)/shard_map/dot_general | solution.py:22
  84.6 0.0 slice-done
  84.6 0.0 slice-done.1
  84.6 4.2 %fusion.8 = f32[256,4608]{1,0:T(8,128)} fusion(bf16[256,640]{1,0:T(8,128)(2,1)S(1)} %all_gather.7, bf16[640,4608]{1,0:T(8,128)(2,1)S(1)} %bitcast.12), kind=kOutput, calls=%fused_computation.13 | convolution fusion | flops 1509949440 | bytes 10944512 | tf_op jit(solution)/shard_map/dot_general | solution.py:40
  88.8 0.0 slice-start.2
  88.8 0.0 all-reduce.3.cloned.1.call-update
  88.8 0.0 reduce-scatter.2.cloned.1.call-start
  88.8 148.5 %all-reduce.3.cloned.1.call-done = (f32[256,4608]{1,0:T(8,128)}, f32[256,4608]{1,0:T(8,128)}) async-done(((f32[256,4608]{1,0:T(8,128)}, f32[256,4608]{1,0:T(8,128)}), (f32[256,4608]{1,0:T(8,128)}, f32[256,4608]{1,0:T(8,128)})) %all-reduce.3.cloned.1.call-update) | async-done | bytes 9437200 | tf_op jit(solution)/shard_map/psum | solution.py:42
  237.3 0.0 slice-start.3
  237.3 4.9 %fusion.6 = bf16[256,4608]{1,0:T(8,128)(2,1)S(1)} fusion(f32[256,4608]{1,0:T(8,128)} %get-tuple-element.6, f32[256,4608]{1,0:T(8,128)} %get-tuple-element.7), kind=kLoop, calls=%fused_computation.9 | loop fusion | flops 11796480 | bytes 11796480 | tf_op jit(solution)/shard_map/convert_element_type | solution.py:30
  242.2 0.0 copy-start
  242.2 1.4 copy-done
  243.6 0.0 slice-done.2
  243.6 0.0 slice-done.3
  243.6 2.9 fusion.9
  246.5 0.0 reduce-scatter.2.cloned.1.call-update
  246.5 6.3 %fusion = bf16[640,4608]{0,1:T(8,128)(2,1)} fusion(bf16[256,4608]{1,0:T(8,128)(2,1)} %copy-done, bf16[256,640]{1,0:T(8,128)(2,1)S(1)} %all_gather.7), kind=kOutput, calls=%fused_computation.2 | convolution fusion | flops 1515847680 | bytes 8585216 | tf_op jit(solution)/shard_map/dot_general | solution.py:16
  252.8 8.9 %copy.7 = bf16[640,4608]{1,0:T(8,128)(2,1)} copy(bf16[640,4608]{0,1:T(8,128)(2,1)} %fusion) | data formatting | bytes 11796480
  261.7 5.9 %multiply_convert_fusion = bf16[4608,640]{1,0:T(8,128)(2,1)} fusion(bf16[256,640]{1,0:T(8,128)(2,1)S(1)} %all_gather.6, f32[256,4608]{1,0:T(8,128)} %get-tuple-element.7), kind=kOutput, calls=%fused_computation | convolution fusion | flops 1521745920 | bytes 10944512 | tf_op jit(solution)/shard_map/dot_general | solution.py:16
  267.6 50.8 %reduce-scatter.2.cloned.1.call-done = f32[32,640]{1,0:T(8,128)} async-done(((f32[256,640]{1,0:T(8,128)}), f32[32,640]{1,0:T(8,128)}) %reduce-scatter.2.cloned.1.call-update) | async-done | bytes 81936 | tf_op jit(solution)/shard_map/reduce_scatter | solution.py:48
  (2 shorter events, 0.0 us)
Async XLA Ops:
  7.2 230.2 %all-reduce.3.cloned.1.call-start = ((), (), s32[]{:S(2)}) async-start(), calls=%async_computation.2 | async-start | bytes 18874368 | tf_op jit(solution)/shard_map/psum | solution.py:42
  42.5 42.0 %slice-start = ((s8[5898240]{0:T(1024)(128)(4,1)}), s8[4194304]{0:T(1024)(128)(4,1)S(1)}, s32[]{:S(2)}) async-start(s8[5898240]{0:T(1024)(128)(4,1)} %bitcast.11), calls=%async_computation.3 | async-start | bytes 8388608
  77.5 7.0 %slice-start.1 = ((s8[5898240]{0:T(1024)(128)(4,1)}), s8[1703936]{0:T(1024)(128)(4,1)S(1)}, s32[]{:S(2)}) async-start(s8[5898240]{0:T(1024)(128)(4,1)} %bitcast.11), calls=%async_computation.4 | async-start | bytes 3407872
  88.8 154.9 %slice-start.2 = ((s8[5898240]{0:T(1024)(128)(4,1)}), s8[1703936]{0:T(1024)(128)(4,1)S(1)}, s32[]{:S(2)}) async-start(s8[5898240]{0:T(1024)(128)(4,1)} %bitcast.13), calls=%async_computation.5 | async-start | bytes 3407872
  88.8 229.7 %reduce-scatter.2.cloned.1.call-start = ((), (), s32[]{:S(2)}) async-start(), calls=%async_computation.1 | async-start | bytes 737280 | tf_op jit(solution)/shard_map/reduce_scatter | solution.py:48
  237.3 6.3 %slice-start.3 = ((s8[5898240]{0:T(1024)(128)(4,1)}), s8[4194304]{0:T(1024)(128)(4,1)S(1)}, s32[]{:S(2)}) async-start(s8[5898240]{0:T(1024)(128)(4,1)} %bitcast.13), calls=%async_computation.6 | async-start | bytes 8388608
  242.2 1.4 copy-start
Sparse Core Ops, SparseCore 0:
  88.9 148.3 all-reduce.2
  246.7 71.7 reduce-scatter.1
where the time goes:
time: 326 us; the launch traced here: 325 us
  waiting for transfers between devices  199 us (61%)
  blocking collectives  70.3 us (22%)
  matrix products  26.3 us (8%)
  between operations  14.1 us (4%)
  local copies, waits for them, and re-layouts  10.3 us (3%)
  other arithmetic  4.88 us (1%)
    psum x1, waiting for transfers between devices, local(): preact, grad_act = lax.psum((partial_pre, partial_grad), 'mp')  148 us
    reduce_scatter x1, waiting for transfers between devices, local(): lax.psum_scatter(partial_all, 'dp', scatter_dimension=0, tiled=True)  50.8 us
    all_gather x1, blocking collectives, local(): lax.all_gather(inputs, 'dp', axis=0, tiled=True)  35.3 us
    all_gather x1, blocking collectives, local(): lax.all_gather(out_grads, 'dp', axis=0, tiled=True)  35 us
    dot_general x2, matrix products, contract_rows(): lax.dot_general(left, right, (((0,), (0,)), ((), ())), preferred_element_...  12.2 us
    unnamed x11, local copies, waits for them, and re-layouts  10.3 us
    dot_general x2, matrix products, contract_cols(): lax.dot_general(left, right, (((1,), (1,)), ((), ())), preferred_element_...  9.9 us
  transfers between devices with their start and end apart: 2, of which 2 were waited for; matrix products, arithmetic and copies ran while one was open for 6% of the time, Pallas kernels for 0%

commit v1 on v0

v1 whole, which is shorter than its diff:
```python
import functools
import math

import jax
import jax.numpy as jnp
from jax import lax
from jax.experimental import pallas as pl
from jax.experimental.pallas import tpu as pltpu
from jax.sharding import PartitionSpec as P

MESH = pl.DeviceIdType.MESH
F32, BF16 = jnp.float32, jnp.bfloat16

NX, NY = 4, 4
GROUPS = 2
LAG1, LAG2, LAG3, LAG4, LAG5, LAG6, LAG7 = 1, 3, 5, 7, 9, 10, 12
SLOTS = 4


def rem(a, b):
    return lax.rem(a, jnp.int32(b))


def div(a, b):
    return lax.div(a, jnp.int32(b))


def mult(v, m):
    return pl.multiple_of(v * m, m)


def dot(a, b):
    return lax.dot_general(a, b, (((1,), (0,)), ((), ())), preferred_element_type=F32)


def dot_nt(a, b):
    return lax.dot_general(a, b, (((1,), (1,)), ((), ())), preferred_element_type=F32)


def dot_tn(a, b):
    return lax.dot_general(a, b, (((0,), (0,)), ((), ())), preferred_element_type=F32)


def gelu_parts(v):
    cumul = 0.5 * (1.0 + lax.erf(v * (1.0 / math.sqrt(2.0))))
    density = jnp.exp(-0.5 * v * v) * (1.0 / math.sqrt(2.0 * math.pi))
    return v * cumul, cumul + v * density


def block_kernel(
    T, D, FC, NF,
    x_hbm, g_hbm, wi_hbm, wo_hbm,
    in_ref, gwi_ref, gwo_ref,
    xg, xt, wi, wo, acc, ag,
    csend, crecv, mine, ysend, yrecv, zmine, zsend, zrecv, dsend, drecv,
    load_sem, wi_sem, wo_sem, a_send, a_recv, i_send, i_recv, d_send, d_recv,
):
    R = NX * T
    H, Q, CB = R // 2, R // 4, FC // NY
    ITEMS = GROUPS * NF
    dp, mp = lax.axis_index("dp"), lax.axis_index("mp")
    x, zhi = div(dp, 2), rem(dp, 2)
    zlo, y, core = div(mp, 8), rem(div(mp, 2), NY), rem(mp, 2)

    def slot_of(j):
        return rem(div(j, 2) + core, 2) * 2 + rem(rem(j, 2) + zlo, 2)

    def mp_peer(dz=0, dy=0, dc=0):
        return (dp, rem(zlo + dz, 2) * 8 + rem(y + dy, NY) * 2 + rem(core + dc, 2))

    def dp_peer(g, k):
        return (rem(x + k, NX) * 2 + rem(zhi + g, 2), mp)

    peers = [mp_peer(dc=1), mp_peer(dz=1)] + [mp_peer(dy=k) for k in range(1, NY)]
    dps = [(g, k) for g in range(GROUPS) for k in range(NX) if g or k]
    barrier = pltpu.get_barrier_semaphore()
    for peer in peers + [dp_peer(g, k) for g, k in dps]:
        pl.semaphore_signal(barrier, inc=1, device_id=peer, device_id_type=MESH)

    own = mult(slot_of(x), T)
    loads = [
        pltpu.make_async_copy(x_hbm, xg.at[0, pl.ds(own, T)], load_sem.at[0]),
        pltpu.make_async_copy(g_hbm, xg.at[1, pl.ds(own, T)], load_sem.at[1]),
    ]
    for c in loads:
        c.start()

    def wi_copy(f):
        cols = pl.ds(mult(f, FC), FC)
        return pltpu.make_async_copy(wi_hbm.at[:, cols], wi.at[:, cols], wi_sem.at[f])

    def wo_copy(f):
        rows = pl.ds(mult(f, FC), FC)
        return pltpu.make_async_copy(wo_hbm.at[rows], wo.at[rows], wo_sem.at[f])

    for f in range(NF):
        wi_copy(f).start()
        wo_copy(f).start()

    def remote(src, dst, send, recv, peer):
        return pltpu.make_async_remote_copy(
            src_ref=src, dst_ref=dst, send_sem=send, recv_sem=recv, device_id=peer, device_id_type=MESH
        )

    def a_copy(i, g, k):
        src = xg.at[:, pl.ds(own, T)]
        dst = xg.at[:, pl.ds(pl.multiple_of(g * R + own, T), T)]
        return remote(src, dst, a_send.at[i], a_recv.at[i], dp_peer(g, k))

    def a_wait(i, g, k):
        land = xg.at[:, pl.ds(pl.multiple_of(g * R + slot_of(rem(x + NX - k, NX)) * T, T), T)]
        remote(land, land, a_send.at[i], a_recv.at[i], dp_peer(g, k)).wait_recv()

    for c in loads:
        c.wait()
    pl.semaphore_wait(barrier, len(peers) + len(dps))
    for i, (g, k) in enumerate(dps):
        a_copy(i, g, k).start()

    def item(t):
        g, f = div(t, NF), rem(t, NF)
        return g, f, pl.multiple_of(g * R, R), pl.multiple_of(f * FC, FC)

    def ycols(base, dy):
        return pl.ds(pl.multiple_of(base + rem(y + dy, NY) * CB, CB), CB)

    def item_copy(t, kind):
        _, _, r0, c0 = item(t)
        name, k = kind
        if name == "c":
            n, src, dst, peer = 0, csend.at[t], crecv.at[t], mp_peer(dc=1)
        elif name == "y":
            n, src, dst, peer = k, ysend.at[t, :, :, ycols(0, k)], yrecv.at[t, k - 1], mp_peer(dy=k)
        elif name == "z":
            n, src, dst, peer = 4, zsend.at[t], zrecv.at[t], mp_peer(dz=1)
        elif name == "Y":
            src = ag.at[:, pl.ds(r0, Q), ycols(c0, 0)]
            n, dst, peer = 4 + k, src, mp_peer(dy=k)
        elif name == "Z":
            n, src, peer = 8, ag.at[:, pl.ds(r0, Q), pl.ds(c0, FC)], mp_peer(dz=1)
            dst = ag.at[:, pl.ds(pl.multiple_of(r0 + Q, Q), Q), pl.ds(c0, FC)]
        else:
            peer = mp_peer(dc=1)
            src = ag.at[:, pl.ds(pl.multiple_of(r0 + k * Q, Q), Q), pl.ds(c0, FC)]
            n, dst = 9 + k, ag.at[:, pl.ds(pl.multiple_of(r0 + H + k * Q, Q), Q), pl.ds(c0, FC)]
        return remote(src, dst, i_send.at[t, n], i_recv.at[t, n], peer)

    def start(t, *kinds):
        for kind in kinds:
            item_copy(t, kind).start()

    def wait_recv(t, *kinds):
        for kind in kinds:
            if kind[0] == "Y":
                _, _, r0, c0 = item(t)
                n = 4 + kind[1]
                land = ag.at[:, pl.ds(r0, Q), ycols(c0, NY - kind[1])]
                remote(land, land, i_send.at[t, n], i_recv.at[t, n], mp_peer(dy=kind[1])).wait_recv()
            else:
                item_copy(t, kind).wait_recv()

    ys = [("y", k) for k in range(1, NY)]
    Ys = [("Y", k) for k in range(1, NY)]

    def stage0(t):
        g, f, r0, c0 = item(t)
        s = rem(t, SLOTS)

        @pl.when(t == 0)
        def _():
            for i, (gg, k) in enumerate(dps):
                if gg == 0:
                    a_wait(i, gg, k)

        @pl.when(t == NF)
        def _():
            for i, (gg, k) in enumerate(dps):
                if gg == 1:
                    a_wait(i, gg, k)
            xt[...] = xg[0].T

        @pl.when(t < NF)
        def _():
            wi_copy(f).wait()
            wo_copy(f).wait()

        pre = dot(xg[0, pl.ds(r0, R)], wi[:, pl.ds(c0, FC)])
        mine[s, 0] = pre[:H]
        csend[t, 0] = pre[H:].astype(BF16)
        grad = dot_nt(xg[1, pl.ds(r0, R)], wo[pl.ds(c0, FC)])
        mine[s, 1] = grad[:H]
        csend[t, 1] = grad[H:].astype(BF16)
        start(t, ("c", 0))

    def stage1(t):
        s = rem(t, SLOTS)
        wait_recv(t, ("c", 0))
        total = mine[s] + crecv[t].astype(F32)
        mine[s] = total
        ysend[t] = total.astype(BF16)
        start(t, *ys)

    def stage2(t):
        s = rem(t, SLOTS)
        wait_recv(t, *ys)
        total = mine[s, :, :, ycols(0, 0)]
        for k in range(NY - 1):
            total = total + yrecv[t, k].astype(F32)
        zmine[s] = total[:, :Q]
        zsend[t] = total[:, Q:].astype(BF16)
        start(t, ("z", 0))

    def stage3(t):
        s = rem(t, SLOTS)
        _, _, r0, c0 = item(t)
        wait_recv(t, ("z", 0))
        total = zmine[s] + zrecv[t].astype(F32)
        value, slope = gelu_parts(total[0])
        ag[0, pl.ds(r0, Q), ycols(c0, 0)] = value.astype(BF16)
        ag[1, pl.ds(r0, Q), ycols(c0, 0)] = (total[1] * slope).astype(BF16)
        start(t, *Ys)

    def stage4(t):
        wait_recv(t, *Ys)
        start(t, ("Z", 0), ("C", 0))

    def stage5(t):
        wait_recv(t, ("Z", 0))
        start(t, ("C", 1))

    def d_copy(i, g, k):
        return remote(dsend.at[i], drecv.at[i], d_send.at[i], d_recv.at[i], dp_peer(g, k))

    def stage6(t):
        g, f, r0, c0 = item(t)
        wait_recv(t, ("C", 0), ("C", 1))
        part = dot_nt(ag[1, pl.ds(r0, R), pl.ds(c0, FC)], wi[:, pl.ds(c0, FC)])

        @pl.when(f == 0)
        def _():
            acc[pl.ds(r0, R)] = part

        @pl.when(f > 0)
        def _():
            acc[pl.ds(r0, R)] += part

        for gg in range(GROUPS):
            @pl.when(t == gg * NF + NF - 1)
            def _():
                for i, (g2, k) in enumerate(dps):
                    if g2 == gg:
                        rows = pl.multiple_of(g2 * R + slot_of(rem(x + k, NX)) * T, T)
                        dsend[i] = acc[pl.ds(rows, T)].astype(BF16)
                        d_copy(i, g2, k).start()

    factor = 1.0 / math.sqrt(GROUPS * R)

    def stage7(t):
        _, _, _, c0 = item(t)
        cols = pl.ds(c0, FC)
        gwi_ref[:, cols] = (dot(xt[...], ag[1, :, cols]) * factor).astype(BF16)
        gwo_ref[cols, :] = (dot_tn(ag[0, :, cols], xg[1]) * factor).astype(BF16)

    stages = [
        (stage5, LAG5, 0), (stage4, LAG4, 0), (stage3, LAG3, 0), (stage2, LAG2, 0), (stage1, LAG1, 0),
        (stage0, 0, 0), (stage6, LAG6, 0), (stage7, LAG7, NF),
    ]

    @pl.loop(0, ITEMS + LAG7)
    def _(tick):
        for stage, lag, first in stages:
            @pl.when(jnp.logical_and(tick >= lag + first, tick < lag + ITEMS))
            def _():
                stage(tick - lag)

    total = acc[pl.ds(own, T)]
    for i, (g, k) in enumerate(dps):
        d_copy(i, g, k).wait_recv()
        total = total + drecv[i].astype(F32)
    in_ref[...] = total

    for i, (g, k) in enumerate(dps):
        a_copy(i, g, k).wait_send()
        d_copy(i, g, k).wait_send()

    @pl.loop(0, ITEMS)
    def _(t):
        for kind in [("c", 0), *ys, ("z", 0), *Ys, ("Z", 0), ("C", 0), ("C", 1)]:
            item_copy(t, kind).wait_send()


def store_kernel(in_ref, gwi_ref, gwo_ref, in_out, gwi_out, gwo_out, sem):
    copies = [
        pltpu.make_async_copy(gwi_ref, gwi_out, sem.at[0]),
        pltpu.make_async_copy(gwo_ref, gwo_out, sem.at[1]),
        pltpu.make_async_copy(in_ref, in_out, sem.at[2]),
    ]
    for c in copies:
        c.start()
    for c in copies:
        c.wait()


def local(inputs, out_grads, w_in, w_out):
    T, D = inputs.shape
    FF = w_in.shape[1]
    FC = 512
    NF = FF // FC
    R = NX * T
    H, Q, CB = R // 2, R // 4, FC // NY
    ITEMS = GROUPS * NF
    TOK = GROUPS * R
    DPS = GROUPS * NX - 1
    vmem = pl.BlockSpec(memory_space=pltpu.VMEM)
    hbm = pl.BlockSpec(memory_space=pl.ANY)
    dma = pltpu.SemaphoreType.DMA
    shapes = [((T, D), F32), ((D, FF), BF16), ((FF, D), BF16)]
    parts = pl.pallas_call(
        functools.partial(block_kernel, T, D, FC, NF),
        out_shape=[pltpu.VMEM(s, d) for s, d in shapes],
        in_specs=[hbm] * 4,
        out_specs=[vmem] * 3,
        scratch_shapes=[
            pltpu.VMEM((2, TOK, D), BF16),
            pltpu.VMEM((D, TOK), BF16),
            pltpu.VMEM((D, FF), BF16),
            pltpu.VMEM((FF, D), BF16),
            pltpu.VMEM((TOK, D), F32),
            pltpu.VMEM((2, TOK, FF), BF16),
            pltpu.VMEM((ITEMS, 2, H, FC), BF16),
            pltpu.VMEM((ITEMS, 2, H, FC), BF16),
            pltpu.VMEM((SLOTS, 2, H, FC), F32),
            pltpu.VMEM((ITEMS, 2, H, FC), BF16),
            pltpu.VMEM((ITEMS, NY - 1, 2, H, CB), BF16),
            pltpu.VMEM((SLOTS, 2, Q, CB), F32),
            pltpu.VMEM((ITEMS, 2, Q, CB), BF16),
            pltpu.VMEM((ITEMS, 2, Q, CB), BF16),
            pltpu.VMEM((DPS, T, D), BF16),
            pltpu.VMEM((DPS, T, D), BF16),
            dma((2,)), dma((NF,)), dma((NF,)),
            dma((DPS,)), dma((DPS,)),
            dma((ITEMS, 11)), dma((ITEMS, 11)),
            dma((DPS,)), dma((DPS,)),
        ],
        compiler_params=pltpu.CompilerParams(
            collective_id=0, has_side_effects=True, vmem_limit_bytes=44 * 2**20
        ),
        name="ffn_backward",
    )(inputs, out_grads, w_in, w_out)
    return pl.pallas_call(
        store_kernel,
        out_shape=[jax.ShapeDtypeStruct(s, d) for s, d in shapes],
        in_specs=[vmem] * 3,
        out_specs=[hbm] * 3,
        scratch_shapes=[dma((3,))],
        compiler_params=pltpu.CompilerParams(vmem_limit_bytes=2**20),
        name="store_results",
    )(*parts)


def solution(mesh):
    return jax.shard_map(
        local,
        mesh=mesh,
        in_specs=(P("dp", "mp"), P("dp", "mp"), P("mp", "dp"), P("dp", "mp")),
        out_specs=(P("dp", "mp"), P("mp", "dp"), P("dp", "mp")),
        check_vma=False,
    )
```

time: 326 us -> 85.5 us (0.26)
  waiting for transfers between devices: 199 us -> 0 us
  Pallas kernels: 0 us -> 84.8 us
  blocking collectives: 70.3 us -> 0 us
  matrix products: 26.3 us -> 0 us
  between operations: 14.1 us -> 0.64 us
  local copies, waits for them, and re-layouts: 10.3 us -> 0 us
  other arithmetic: 4.88 us -> 0 us
    psum x1 -> x0, waiting for transfers between devices: 148 us -> none  [local(): preact, grad_act = lax.psum((partial_pre, partial_grad), 'mp')]
    pallas_call x0 -> x2, Pallas kernels: none -> 84.8 us  [the longest x1 80.2 us: local(): pl.pallas_call(functools.partial(block_kernel, T, D, FC, NF), out_shape=[...]
    all_gather x2 -> x0, blocking collectives: 70.3 us -> none  [the longest x1 35.3 us: local(): lax.all_gather(inputs, 'dp', axis=0, tiled=True)]
    reduce_scatter x1 -> x0, waiting for transfers between devices: 50.8 us -> none  [local(): lax.psum_scatter(partial_all, 'dp', scatter_dimension=0, tiled=True)]
    dot_general x5 -> x0, matrix products: 26.3 us -> none  [the longest x2 12.2 us: contract_rows(): lax.dot_general(left, right, (((0,), (0,)), ((), ())), preferred_element_...]
    unnamed x11 -> x0, local copies, waits for them, and re-layouts: 10.3 us -> none
    convert_element_type x1 -> x0, other arithmetic: 4.88 us -> none  [finish(): grad_preact = (grad_act * gelu_slope).astype(jnp.bfloat16)]
  transfers between devices with their start and end apart: 2 -> 0, of which waited for: 2 -> 0; matrix products, arithmetic and copies ran while one was open for 6% -> 0% of each run, Pallas kernels for 0% -> 0%
where the time goes in v1:
time: 85.5 us; the launch traced here: 85.4 us
  Pallas kernels  84.8 us (99%)
    pallas_call x1, Pallas kernels, local(): pl.pallas_call(functools.partial(block_kernel, T, D, FC, NF), out_shape=[...  80.2 us
    pallas_call x1, Pallas kernels, local(): pl.pallas_call(store_kernel, out_shape=[jax.ShapeDtypeStruct(s, d) for s,...  4.54 us

profile of v1, /device:TPU:0, one launch (start us, length us, event | category | flops | bytes accessed | tf_op | source)
XLA Modules:
  0.0 85.4 jit_solution(9811519895068118554)
XLA Ops:
  0.6 80.2 %ffn_backward.1 = (f32[32,640]{1,0:T(8,128)S(1)}, bf16[640,4608]{1,0:T(8,128)(2,1)S(1)}, bf16[4608,640]{1,0:T(8,128)(2,1)S(1)}) custom-call(bf16[32,640]{1,0:T(8,128)(2,1)} %x_hbm.1, bf16[32,640]{1,0:T(8,128)(2,1)} %g_hbm.1, bf16[640,4608]{1,0:T(8,128)(2,1)} %wi_hbm.1, bf16[4608,640]{1,0:T(8,128)(2,1)} %wo_hbm.1), custom_call_target="tpu_custom_call" | custom-call | tf_op jit(solution)/shard_map/ffn_backward/pallas_call | solution.py:318
  80.9 4.5 %store_results.1 = (f32[32,640]{1,0:T(8,128)}, bf16[640,4608]{1,0:T(8,128)(2,1)}, bf16[4608,640]{1,0:T(8,128)(2,1)}) custom-call(f32[32,640]{1,0:T(8,128)S(1)} %get-tuple-element.6.in_ref, bf16[640,4608]{1,0:T(8,128)(2,1)S(1)} %get-tuple-element.7.gwi_ref, bf16[4608,640]{1,0:T(8,128)(2,1)S(1)} %get-tuple-element.8.gwo_ref), custom_call_target="tpu_custom_call" | custom-call | tf_op jit(solution)/shard_map/store_results/pallas_call | solution.py:350

commit v2 on v1

--- a/solution.py
+++ b/solution.py
@@ -13,8 +13,10 @@
 
 NX, NY = 4, 4
 GROUPS = 2
-LAG1, LAG2, LAG3, LAG4, LAG5, LAG6, LAG7 = 1, 3, 5, 7, 9, 10, 12
-SLOTS = 4
+LAGS = (0, 3, 8, 13, 18, 22, 26, 30, 32, 34)
+SLOTS = 24
+ODD_FROM, ODD_TO = 2, 14
+NAMES = ("c", "y+", "y-", "r+", "r-", "z", "Z", "Y+", "Y-", "R+", "R-", "C")
 
 
 def rem(a, b):
@@ -52,7 +54,7 @@
     x_hbm, g_hbm, wi_hbm, wo_hbm,
     in_ref, gwi_ref, gwo_ref,
     xg, xt, wi, wo, acc, ag,
-    csend, crecv, mine, ysend, yrecv, zmine, zsend, zrecv, dsend, drecv,
+    csend, crecv, mine, yp, ym, yq, rp, rm, rq, yown, yrel, zmine, qkeep, zs, zr, dsend, drecv,
     load_sem, wi_sem, wo_sem, a_send, a_recv, i_send, i_recv, d_send, d_recv,
 ):
     R = NX * T
@@ -103,19 +105,30 @@
         )
 
     def a_copy(i, g, k):
-        src = xg.at[:, pl.ds(own, T)]
+        src = xg.at[:, pl.ds(pl.multiple_of((R if k and g else 0) + own, T), T)]
         dst = xg.at[:, pl.ds(pl.multiple_of(g * R + own, T), T)]
-        return remote(src, dst, a_send.at[i], a_recv.at[i], dp_peer(g, k))
-
-    def a_wait(i, g, k):
         land = xg.at[:, pl.ds(pl.multiple_of(g * R + slot_of(rem(x + NX - k, NX)) * T, T), T)]
-        remote(land, land, a_send.at[i], a_recv.at[i], dp_peer(g, k)).wait_recv()
+        peer = dp_peer(0, k) if k else dp_peer(g, 0)
+        return remote(src, dst, a_send.at[i], a_recv.at[i], peer), remote(land, land, a_send.at[i], a_recv.at[i], peer)
+
+    def gather_start(pick):
+        for i, (g, k) in enumerate(dps):
+            if pick(g, k):
+                a_copy(i, g, k)[0].start()
+
+    def gather_wait(pick):
+        for i, (g, k) in enumerate(dps):
+            if pick(g, k):
+                a_copy(i, g, k)[1].wait_recv()
 
     for c in loads:
         c.wait()
     pl.semaphore_wait(barrier, len(peers) + len(dps))
-    for i, (g, k) in enumerate(dps):
-        a_copy(i, g, k).start()
+    gather_start(lambda g, k: g == 0)
+    gather_start(lambda g, k: k == 0)
+
+    def is_odd(t):
+        return jnp.logical_and(rem(t, 2) == 0, jnp.logical_and(t >= ODD_FROM, t <= ODD_TO))
 
     def item(t):
         g, f = div(t, NF), rem(t, NF)
@@ -124,59 +137,73 @@
     def ycols(base, dy):
         return pl.ds(pl.multiple_of(base + rem(y + dy, NY) * CB, CB), CB)
 
-    def item_copy(t, kind):
+    def item_copy(t, odd, name):
         _, _, r0, c0 = item(t)
-        name, k = kind
+        rows = Q if odd else H
+        n = NAMES.index(name)
+        up, down, zp, cp = mp_peer(dy=1), mp_peer(dy=NY - 1), mp_peer(dz=1), mp_peer(dc=1)
+        head, own_z, other_z = pl.ds(0, rows), pl.ds(r0, Q), pl.ds(pl.multiple_of(r0 + Q, Q), Q)
+        gather = pl.ds(r0, rows)
+        zcols = pl.ds(0, FC if odd else CB)
         if name == "c":
-            n, src, dst, peer = 0, csend.at[t], crecv.at[t], mp_peer(dc=1)
-        elif name == "y":
-            n, src, dst, peer = k, ysend.at[t, :, :, ycols(0, k)], yrecv.at[t, k - 1], mp_peer(dy=k)
+            src, dst, peer = csend.at[t], crecv.at[t], cp
+        elif name == "y+":
+            src, dst, peer = yp.at[t, :, head], rp.at[t, :, head], up
+        elif name == "y-":
+            src, dst, peer = ym.at[t, :, head], rm.at[t, :, head], down
+        elif name == "r+":
+            src, dst, peer = yq.at[t, 0, head], rq.at[t, 0, head], up
+        elif name == "r-":
+            src, dst, peer = yq.at[t, 1, head], rq.at[t, 1, head], down
         elif name == "z":
-            n, src, dst, peer = 4, zsend.at[t], zrecv.at[t], mp_peer(dz=1)
-        elif name == "Y":
-            src = ag.at[:, pl.ds(r0, Q), ycols(c0, 0)]
-            n, dst, peer = 4 + k, src, mp_peer(dy=k)
+            src, dst, peer = zs.at[t, :, :, zcols], zr.at[t, :, :, zcols], zp
         elif name == "Z":
-            n, src, peer = 8, ag.at[:, pl.ds(r0, Q), pl.ds(c0, FC)], mp_peer(dz=1)
-            dst = ag.at[:, pl.ds(pl.multiple_of(r0 + Q, Q), Q), pl.ds(c0, FC)]
+            zc = pl.ds(c0, FC) if odd else ycols(c0, 0)
+            src, dst, peer = ag.at[:, own_z, zc], ag.at[:, other_z, zc], zp
+        elif name == "Y+":
+            src, peer = ag.at[:, gather, ycols(c0, 0)], up
+            dst, land = src, ag.at[:, gather, ycols(c0, NY - 1)]
+        elif name == "Y-":
+            src, peer = ag.at[:, gather, ycols(c0, 0)], down
+            dst, land = src, ag.at[:, gather, ycols(c0, 1)]
+        elif name == "R+":
+            src, peer = ag.at[0, gather, ycols(c0, NY - 1)], up
+            dst, land = src, ag.at[0, gather, ycols(c0, 2)]
+        elif name == "R-":
+            src, peer = ag.at[1, gather, ycols(c0, 1)], down
+            dst, land = src, ag.at[1, gather, ycols(c0, 2)]
         else:
-            peer = mp_peer(dc=1)
-            src = ag.at[:, pl.ds(pl.multiple_of(r0 + k * Q, Q), Q), pl.ds(c0, FC)]
-            n, dst = 9 + k, ag.at[:, pl.ds(pl.multiple_of(r0 + H + k * Q, Q), Q), pl.ds(c0, FC)]
-        return remote(src, dst, i_send.at[t, n], i_recv.at[t, n], peer)
-
-    def start(t, *kinds):
-        for kind in kinds:
-            item_copy(t, kind).start()
-
-    def wait_recv(t, *kinds):
-        for kind in kinds:
-            if kind[0] == "Y":
-                _, _, r0, c0 = item(t)
-                n = 4 + kind[1]
-                land = ag.at[:, pl.ds(r0, Q), ycols(c0, NY - kind[1])]
-                remote(land, land, i_send.at[t, n], i_recv.at[t, n], mp_peer(dy=kind[1])).wait_recv()
-            else:
-                item_copy(t, kind).wait_recv()
-
-    ys = [("y", k) for k in range(1, NY)]
-    Ys = [("Y", k) for k in range(1, NY)]
-
-    def stage0(t):
+            src, peer = ag.at[:, pl.ds(r0, H), pl.ds(c0, FC)], cp
+            dst = ag.at[:, pl.ds(pl.multiple_of(r0 + H, H), H), pl.ds(c0, FC)]
+        if name not in ("Y+", "Y-", "R+", "R-"):
+            land = dst
+        send, recv = i_send.at[t, n], i_recv.at[t, n]
+        return remote(src, dst, send, recv, peer), remote(land, land, send, recv, peer)
+
+    def start(t, odd, *names):
+        for name in names:
+            item_copy(t, odd, name)[0].start()
+
+    def wait(t, odd, *names):
+        for name in names:
+            item_copy(t, odd, name)[1].wait_recv()
+
+    def products(t):
         g, f, r0, c0 = item(t)
         s = rem(t, SLOTS)
 
         @pl.when(t == 0)
         def _():
-            for i, (gg, k) in enumerate(dps):
-                if gg == 0:
-                    a_wait(i, gg, k)
+            gather_wait(lambda g, k: g == 0)
+
+        @pl.when(t == 1)
+        def _():
+            gather_wait(lambda g, k: k == 0)
+            gather_start(lambda g, k: g and k)
 
         @pl.when(t == NF)
         def _():
-            for i, (gg, k) in enumerate(dps):
-                if gg == 1:
-                    a_wait(i, gg, k)
+            gather_wait(lambda g, k: g and k)
             xt[...] = xg[0].T
 
         @pl.when(t < NF)
@@ -190,50 +217,106 @@
         grad = dot_nt(xg[1, pl.ds(r0, R)], wo[pl.ds(c0, FC)])
         mine[s, 1] = grad[:H]
         csend[t, 1] = grad[H:].astype(BF16)
-        start(t, ("c", 0))
-
-    def stage1(t):
-        s = rem(t, SLOTS)
-        wait_recv(t, ("c", 0))
-        total = mine[s] + crecv[t].astype(F32)
-        mine[s] = total
-        ysend[t] = total.astype(BF16)
-        start(t, *ys)
-
-    def stage2(t):
-        s = rem(t, SLOTS)
-        wait_recv(t, *ys)
-        total = mine[s, :, :, ycols(0, 0)]
-        for k in range(NY - 1):
-            total = total + yrecv[t, k].astype(F32)
-        zmine[s] = total[:, :Q]
-        zsend[t] = total[:, Q:].astype(BF16)
-        start(t, ("z", 0))
-
-    def stage3(t):
-        s = rem(t, SLOTS)
+        start(t, 0, "c")
+
+    def y_first(t, odd, block):
+        s, n = rem(t, SLOTS), Q if odd else H
+        yown[s, :, :n] = block(0)
+        b = block(1)
+        yrel[s, 0, :n] = b[0]
+        yp[t, 1, :n] = b[1].astype(BF16)
+        b = block(2)
+        yp[t, 0, :n] = b[0].astype(BF16)
+        start(t, odd, "y+")
+        ym[t, 1, :n] = b[1].astype(BF16)
+        b = block(3)
+        yrel[s, 1, :n] = b[1]
+        ym[t, 0, :n] = b[0].astype(BF16)
+        start(t, odd, "y-")
+
+    def y_relay(t, odd):
+        s, n = rem(t, SLOTS), Q if odd else H
+        wait(t, odd, "y+", "y-")
+        yq[t, 0, :n] = (yrel[s, 0, :n] + rp[t, 0, :n].astype(F32)).astype(BF16)
+        start(t, odd, "r+")
+        yq[t, 1, :n] = (yrel[s, 1, :n] + rm[t, 1, :n].astype(F32)).astype(BF16)
+        start(t, odd, "r-")
+        yown[s, 0, :n] += rm[t, 0, :n].astype(F32)
+        yown[s, 1, :n] += rp[t, 1, :n].astype(F32)
+
+    def y_last(t, odd):
+        s, n = rem(t, SLOTS), Q if odd else H
+        wait(t, odd, "r+", "r-")
+        return yown[s, :, :n] + rq[t, :, :n].astype(F32)
+
+    def gelu(t, total):
         _, _, r0, c0 = item(t)
-        wait_recv(t, ("z", 0))
-        total = zmine[s] + zrecv[t].astype(F32)
         value, slope = gelu_parts(total[0])
         ag[0, pl.ds(r0, Q), ycols(c0, 0)] = value.astype(BF16)
         ag[1, pl.ds(r0, Q), ycols(c0, 0)] = (total[1] * slope).astype(BF16)
-        start(t, *Ys)
-
-    def stage4(t):
-        wait_recv(t, *Ys)
-        start(t, ("Z", 0), ("C", 0))
-
-    def stage5(t):
-        wait_recv(t, ("Z", 0))
-        start(t, ("C", 1))
+
+    def even1(t):
+        s = rem(t, SLOTS)
+        wait(t, 0, "c")
+        y_first(t, 0, lambda dy: mine[s, :, :, ycols(0, dy)] + crecv[t, :, :, ycols(0, dy)].astype(F32))
+
+    def even3(t):
+        s = rem(t, SLOTS)
+        total = y_last(t, 0)
+        zmine[s] = total[:, :Q]
+        zs[t, :, :, :CB] = total[:, Q:].astype(BF16)
+        start(t, 0, "z")
+
+    def even4(t):
+        s = rem(t, SLOTS)
+        wait(t, 0, "z")
+        gelu(t, zmine[s] + zr[t, :, :, :CB].astype(F32))
+        start(t, 0, "Z")
+
+    def even5(t):
+        wait(t, 0, "Z")
+        start(t, 0, "Y+", "Y-")
+
+    def odd1(t):
+        s = rem(t, SLOTS)
+        wait(t, 1, "c")
+        zs[t] = (mine[s, :, Q:] + crecv[t, :, Q:].astype(F32)).astype(BF16)
+        start(t, 1, "z")
+        qkeep[s] = mine[s, :, :Q] + crecv[t, :, :Q].astype(F32)
+
+    def odd2(t):
+        s = rem(t, SLOTS)
+        wait(t, 1, "z")
+        y_first(t, 1, lambda dy: qkeep[s, :, :, ycols(0, dy)] + zr[t, :, :, ycols(0, dy)].astype(F32))
+
+    def odd4(t):
+        gelu(t, y_last(t, 1))
+        start(t, 1, "Y+", "Y-")
+
+    def y_forward(t, odd):
+        wait(t, odd, "Y+")
+        start(t, odd, "R+")
+        wait(t, odd, "Y-")
+        start(t, odd, "R-")
+
+    def even7(t):
+        wait(t, 0, "R+", "R-")
+        start(t, 0, "C")
+
+    def odd6(t):
+        wait(t, 1, "R+", "R-")
+        start(t, 1, "Z")
+
+    def odd7(t):
+        wait(t, 1, "Z")
+        start(t, 1, "C")
 
     def d_copy(i, g, k):
         return remote(dsend.at[i], drecv.at[i], d_send.at[i], d_recv.at[i], dp_peer(g, k))
 
-    def stage6(t):
+    def hidden_sum(t):
         g, f, r0, c0 = item(t)
-        wait_recv(t, ("C", 0), ("C", 1))
+        wait(t, 0, "C")
         part = dot_nt(ag[1, pl.ds(r0, R), pl.ds(c0, FC)], wi[:, pl.ds(c0, FC)])
 
         @pl.when(f == 0)
@@ -255,23 +338,34 @@
 
     factor = 1.0 / math.sqrt(GROUPS * R)
 
-    def stage7(t):
+    def weight_grads(t):
         _, _, _, c0 = item(t)
         cols = pl.ds(c0, FC)
         gwi_ref[:, cols] = (dot(xt[...], ag[1, :, cols]) * factor).astype(BF16)
         gwo_ref[cols, :] = (dot_tn(ag[0, :, cols], xg[1]) * factor).astype(BF16)
 
-    stages = [
-        (stage5, LAG5, 0), (stage4, LAG4, 0), (stage3, LAG3, 0), (stage2, LAG2, 0), (stage1, LAG1, 0),
-        (stage0, 0, 0), (stage6, LAG6, 0), (stage7, LAG7, NF),
+    both = [
+        (even7, odd7), (lambda t: y_forward(t, 0), odd6), (even5, lambda t: y_forward(t, 1)), (even4, odd4),
+        (even3, lambda t: y_relay(t, 1)), (lambda t: y_relay(t, 0), odd2), (even1, odd1),
     ]
 
-    @pl.loop(0, ITEMS + LAG7)
+    @pl.loop(0, ITEMS + LAGS[9])
     def _(tick):
-        for stage, lag, first in stages:
-            @pl.when(jnp.logical_and(tick >= lag + first, tick < lag + ITEMS))
+        def at(lag, first, run, other=None):
+            t = tick - lag
+
+            @pl.when(jnp.logical_and(t >= first, t < ITEMS))
             def _():
-                stage(tick - lag)
+                if other is None:
+                    run(t)
+                else:
+                    lax.cond(is_odd(t), lambda: other(t), lambda: run(t))
+
+        for n, (even, odd) in zip(range(7, 0, -1), both):
+            at(LAGS[n], 0, even, odd)
+        at(0, 0, products)
+        at(LAGS[8], 0, hidden_sum)
+        at(LAGS[9], NF, weight_grads)
 
     total = acc[pl.ds(own, T)]
     for i, (g, k) in enumerate(dps):
@@ -280,13 +374,16 @@
     in_ref[...] = total
 
     for i, (g, k) in enumerate(dps):
-        a_copy(i, g, k).wait_send()
+        a_copy(i, g, k)[0].wait_send()
         d_copy(i, g, k).wait_send()
 
     @pl.loop(0, ITEMS)
     def _(t):
-        for kind in [("c", 0), *ys, ("z", 0), *Ys, ("Z", 0), ("C", 0), ("C", 1)]:
-            item_copy(t, kind).wait_send()
+        for odd in range(2):
+            @pl.when(is_odd(t) if odd else jnp.logical_not(is_odd(t)))
+            def _():
+                for name in NAMES:
+                    item_copy(t, odd, name)[0].wait_send()
 
 
 def store_kernel(in_ref, gwi_ref, gwo_ref, in_out, gwi_out, gwo_out, sem):
@@ -330,16 +427,16 @@
             pltpu.VMEM((ITEMS, 2, H, FC), BF16),
             pltpu.VMEM((ITEMS, 2, H, FC), BF16),
             pltpu.VMEM((SLOTS, 2, H, FC), F32),
-            pltpu.VMEM((ITEMS, 2, H, FC), BF16),
-            pltpu.VMEM((ITEMS, NY - 1, 2, H, CB), BF16),
+            *[pltpu.VMEM((ITEMS, 2, H, CB), BF16)] * 6,
+            *[pltpu.VMEM((SLOTS, 2, H, CB), F32)] * 2,
             pltpu.VMEM((SLOTS, 2, Q, CB), F32),
-            pltpu.VMEM((ITEMS, 2, Q, CB), BF16),
-            pltpu.VMEM((ITEMS, 2, Q, CB), BF16),
+            pltpu.VMEM((SLOTS, 2, Q, FC), F32),
+            *[pltpu.VMEM((ITEMS, 2, Q, FC), BF16)] * 2,
             pltpu.VMEM((DPS, T, D), BF16),
             pltpu.VMEM((DPS, T, D), BF16),
             dma((2,)), dma((NF,)), dma((NF,)),
             dma((DPS,)), dma((DPS,)),
-            dma((ITEMS, 11)), dma((ITEMS, 11)),
+            dma((ITEMS, len(NAMES))), dma((ITEMS, len(NAMES))),
             dma((DPS,)), dma((DPS,)),
         ],
         compiler_params=pltpu.CompilerParams(

time: 85.5 us -> 76.6 us (0.90)
  Pallas kernels: 84.8 us -> 75.9 us
    pallas_call x1, Pallas kernels: 80.2 us -> 71.3 us  [local(): pl.pallas_call(functools.partial(block_kernel, T, D, FC, NF), out_shape=[...]
where the time goes in v2:
time: 76.6 us; the launch traced here: 76.5 us
  Pallas kernels  75.9 us (99%)
    pallas_call x1, Pallas kernels, local(): pl.pallas_call(functools.partial(block_kernel, T, D, FC, NF), out_shape=[...  71.3 us
    pallas_call x1, Pallas kernels, local(): pl.pallas_call(store_kernel, out_shape=[jax.ShapeDtypeStruct(s, d) for s,...  4.54 us

profile of v2, /device:TPU:0, one launch (start us, length us, event | category | flops | bytes accessed | tf_op | source)
XLA Modules:
  0.0 76.5 jit_solution(5313274437207293862)
XLA Ops:
  0.6 71.3 %ffn_backward.1 = (f32[32,640]{1,0:T(8,128)S(1)}, bf16[640,4608]{1,0:T(8,128)(2,1)S(1)}, bf16[4608,640]{1,0:T(8,128)(2,1)S(1)}) custom-call(bf16[32,640]{1,0:T(8,128)(2,1)} %x_hbm.1, bf16[32,640]{1,0:T(8,128)(2,1)} %g_hbm.1, bf16[640,4608]{1,0:T(8,128)(2,1)} %wi_hbm.1, bf16[4608,640]{1,0:T(8,128)(2,1)} %wo_hbm.1), custom_call_target="tpu_custom_call" | custom-call | tf_op jit(solution)/shard_map/ffn_backward/pallas_call | solution.py:415
  72.0 4.5 %store_results.1 = (f32[32,640]{1,0:T(8,128)}, bf16[640,4608]{1,0:T(8,128)(2,1)}, bf16[4608,640]{1,0:T(8,128)(2,1)}) custom-call(f32[32,640]{1,0:T(8,128)S(1)} %get-tuple-element.6.in_ref, bf16[640,4608]{1,0:T(8,128)(2,1)S(1)} %get-tuple-element.7.gwi_ref, bf16[4608,640]{1,0:T(8,128)(2,1)S(1)} %get-tuple-element.8.gwo_ref), custom_call_target="tpu_custom_call" | custom-call | tf_op jit(solution)/shard_map/store_results/pallas_call | solution.py:447

commit v3 on v0

v3 whole, which is shorter than its diff:
```python
import functools
import math

import jax
import jax.numpy as jnp
from jax import lax
from jax.experimental import pallas as pl
from jax.experimental.pallas import tpu as pltpu
from jax.sharding import PartitionSpec as P

MESH = pl.DeviceIdType.MESH
F32, BF16 = jnp.float32, jnp.bfloat16

NX, NY = 4, 4
FACTOR = 1.0 / math.sqrt(256)
GROUPS = 2
COLS = 512
ITEMS = (
    (0, 0, 3, 1),
    (0, 3, 3, 0),
    (0, 6, 3, 0),
    (1, 0, 2, 1),
    (1, 2, 3, 0),
    (1, 5, 2, 1),
    (1, 7, 2, 0),
)
ORDER = (
    (0, 0), (1, 0), (0, 1), (2, 0), (1, 1), (3, 0), (2, 1), (4, 0), (3, 1), (1, 2),
    (0, 2), (5, 0), (4, 1), (2, 2), (6, 0), (5, 1), (3, 2), (1, 3), (0, 3), (6, 1),
    (4, 2), (2, 3), (3, 3), (0, 4), (0, 9), (5, 2), (6, 2), (1, 4), (1, 9), (4, 3),
    (2, 4), (3, 4), (0, 5), (3, 9), (2, 9), (0, 10), (5, 3), (1, 5), (1, 10), (6, 3),
    (3, 5), (0, 6), (4, 4), (4, 9), (3, 10), (2, 5), (0, 11), (5, 4), (5, 9), (2, 10),
    (6, 4), (1, 6), (6, 9), (1, 11), (3, 6), (3, 11), (0, 7), (2, 6), (4, 5), (5, 5),
    (4, 10), (5, 10), (0, 8), (2, 11), (1, 7), (0, 12), (1, 12), (6, 5), (2, 7), (6, 10),
    (1, 8), (5, 6), (4, 6), (1, 13), (0, 13), (3, 7), (2, 8), (5, 11), (4, 11), (3, 8),
    (3, 12), (2, 12), (6, 6), (3, 14), (6, 11), (5, 7), (4, 7), (3, 13), (2, 13), (3, 15),
    (6, 7), (5, 8), (4, 8), (6, 12), (5, 12), (6, 8), (4, 12), (4, 14), (6, 13), (5, 13),
    (5, 14), (4, 13), (6, 14), (4, 15),
)
STORED_LATE = 4
SUMS = ("c", "y+", "y-", "r+", "r-", "z")
GATHERS = tuple((name, a) for a in range(2) for name in ("Z", "Y+", "Y-", "R+", "R-", "C"))
NAMES = SUMS + GATHERS


def rem(a, b):
    return lax.rem(a, jnp.int32(b))


def div(a, b):
    return lax.div(a, jnp.int32(b))


def mult(v, m):
    return pl.multiple_of(v * m, m)


def dot(a, b):
    return lax.dot_general(a, b, (((1,), (0,)), ((), ())), preferred_element_type=F32)


def dot_nt(a, b):
    return lax.dot_general(a, b, (((1,), (1,)), ((), ())), preferred_element_type=F32)


def dot_tn(a, b):
    return lax.dot_general(a, b, (((0,), (0,)), ((), ())), preferred_element_type=F32)


def gelu_parts(v):
    cumul = 0.5 * (1.0 + lax.erf(v * (1.0 / math.sqrt(2.0))))
    density = jnp.exp(-0.5 * v * v) * (1.0 / math.sqrt(2.0 * math.pi))
    return v * cumul, cumul + v * density


def block_kernel(
    T, D, NF,
    x_hbm, g_hbm, wi_hbm, wo_hbm,
    in_ref, gwi_ref, gwo_ref, xg, ag,
    xt, wi, wo, acc,
    csend, crecv, mine, yp, ym, yq, rp, rm, rq, yown, yrel, zmine, zs, zr, zsw, zrw, dsend, drecv,
    load_sem, wi_sem, wo_sem, a_send, a_recv, i_send, i_recv, d_send, d_recv,
):
    R = NX * T
    H, Q = R // 2, R // 4
    dp, mp = lax.axis_index("dp"), lax.axis_index("mp")
    x, zhi = div(dp, 2), rem(dp, 2)
    zlo, y, core = div(mp, 8), rem(div(mp, 2), NY), rem(mp, 2)

    def slot_of(j):
        return rem(div(j, 2) + core, 2) * 2 + rem(rem(j, 2) + zlo, 2)

    def mp_peer(dz=0, dy=0, dc=0):
        return (dp, rem(zlo + dz, 2) * 8 + rem(y + dy, NY) * 2 + rem(core + dc, 2))

    def dp_peer(g, k):
        return (rem(x + k, NX) * 2 + rem(zhi + g, 2), mp)

    peers = [mp_peer(dc=1), mp_peer(dz=1)] + [mp_peer(dy=k) for k in range(1, NY)]
    dps = [(g, k) for g in range(GROUPS) for k in range(NX) if g or k]
    barrier = pltpu.get_barrier_semaphore()
    for peer in peers + [dp_peer(g, k) for g, k in dps]:
        pl.semaphore_signal(barrier, inc=1, device_id=peer, device_id_type=MESH)

    own = mult(slot_of(x), T)
    loads = [
        pltpu.make_async_copy(x_hbm, xg.at[0, pl.ds(own, T)], load_sem.at[0]),
        pltpu.make_async_copy(g_hbm, xg.at[1, pl.ds(own, T)], load_sem.at[1]),
    ]
    for c in loads:
        c.start()

    def wi_copy(f):
        cols = pl.ds(f * COLS, COLS)
        return pltpu.make_async_copy(wi_hbm.at[:, cols], wi.at[:, cols], wi_sem.at[f])

    def wo_copy(f):
        rows = pl.ds(f * COLS, COLS)
        return pltpu.make_async_copy(wo_hbm.at[rows], wo.at[rows], wo_sem.at[f])

    for f in range(NF):
        wi_copy(f).start()
        wo_copy(f).start()

    def remote(src, dst, send, recv, peer):
        return pltpu.make_async_remote_copy(
            src_ref=src, dst_ref=dst, send_sem=send, recv_sem=recv, device_id=peer, device_id_type=MESH
        )

    def a_copy(i, g, k):
        src = xg.at[:, pl.ds(pl.multiple_of((R if k and g else 0) + own, T), T)]
        dst = xg.at[:, pl.ds(pl.multiple_of(g * R + own, T), T)]
        land = xg.at[:, pl.ds(pl.multiple_of(g * R + slot_of(rem(x + NX - k, NX)) * T, T), T)]
        peer = dp_peer(0, k) if k else dp_peer(g, 0)
        return remote(src, dst, a_send.at[i], a_recv.at[i], peer), remote(land, land, a_send.at[i], a_recv.at[i], peer)

    def gather_start(pick):
        for i, (g, k) in enumerate(dps):
            if pick(g, k):
                a_copy(i, g, k)[0].start()

    def gather_wait(pick):
        for i, (g, k) in enumerate(dps):
            if pick(g, k):
                a_copy(i, g, k)[1].wait_recv()

    for c in loads:
        c.wait()
    pl.semaphore_wait(barrier, len(peers) + len(dps))
    gather_start(lambda g, k: g == 0)
    gather_start(lambda g, k: k == 0)

    class Item:
        def __init__(self, i):
            g, f, n, self.odd = ITEMS[i]
            self.i, self.g, self.f, self.n = i, g, f, n
            self.r0, self.c0, self.width = g * R, f * COLS, n * COLS
            self.block = self.width // NY
            self.cols = pl.ds(self.c0, self.width)
            self.bcols = pl.ds(self.c0 // NY, self.block)
            self.rows = Q if self.odd else H

        def ycols(self, dy):
            start = self.c0 + rem(y + dy, NY) * self.block
            return pl.ds(pl.multiple_of(start, 128), self.block)

    def item_copy(it, name):
        g, r0, bc, n = it.g, it.r0, it.bcols, NAMES.index(name)
        up, down, zp, cp = mp_peer(dy=1), mp_peer(dy=NY - 1), mp_peer(dz=1), mp_peer(dc=1)
        head, own_z, other_z, gather = pl.ds(0, it.rows), pl.ds(r0, Q), pl.ds(r0 + Q, Q), pl.ds(r0, it.rows)
        land = None
        if name == "c":
            src, dst, peer = csend.at[g, :, :, it.cols], crecv.at[g, :, :, it.cols], cp
        elif name == "y+":
            src, dst, peer = yp.at[g, :, head, bc], rp.at[g, :, head, bc], up
        elif name == "y-":
            src, dst, peer = ym.at[g, :, head, bc], rm.at[g, :, head, bc], down
        elif name == "r+":
            src, dst, peer = yq.at[g, 0, head, bc], rq.at[g, 0, head, bc], up
        elif name == "r-":
            src, dst, peer = yq.at[g, 1, head, bc], rq.at[g, 1, head, bc], down
        elif name == "z" and it.odd:
            src, dst, peer = zsw.at[g, :, :, it.cols], zrw.at[g, :, :, it.cols], zp
        elif name == "z":
            src, dst, peer = zs.at[g, :, :, bc], zr.at[g, :, :, bc], zp
        else:
            name, a = name
            half = it.rows // 2
            if name == "Z":
                zc = it.cols if it.odd else it.ycols(0)
                src, dst, peer = ag.at[a, own_z, zc], ag.at[a, other_z, zc], zp
            elif name == "Y+":
                src = dst = ag.at[a, gather, it.ycols(0)]
                land, peer = ag.at[a, gather, it.ycols(NY - 1)], up
            elif name == "Y-":
                src = dst = ag.at[a, gather, it.ycols(0)]
                land, peer = ag.at[a, gather, it.ycols(1)], down
            elif name == "R+":
                src = dst = ag.at[a, pl.ds(r0, half), it.ycols(NY - 1)]
                land, peer = ag.at[a, pl.ds(r0, half), it.ycols(2)], up
            elif name == "R-":
                src = dst = ag.at[a, pl.ds(r0 + half, half), it.ycols(1)]
                land, peer = ag.at[a, pl.ds(r0 + half, half), it.ycols(2)], down
            else:
                src, dst, peer = ag.at[a, pl.ds(r0, H), it.cols], ag.at[a, pl.ds(r0 + H, H), it.cols], cp
        land = dst if land is None else land
        send, recv = i_send.at[it.i, n], i_recv.at[it.i, n]
        return src, dst, land, send, recv, peer

    def start(it, *names):
        for name in names:
            src, dst, _, send, recv, peer = item_copy(it, name)
            remote(src, dst, send, recv, peer).start()

    def wait(it, *names):
        for name in names:
            _, _, land, send, recv, peer = item_copy(it, name)
            remote(land, land, send, recv, peer).wait_recv()

    def products(it):
        if it.i == 0:
            gather_wait(lambda g, k: g == 0)
        if it.i == 1:
            gather_wait(lambda g, k: k == 0)
            gather_start(lambda g, k: g and k)
        if it.g == 1 and it.f == 0:
            gather_wait(lambda g, k: g and k)
            xt[...] = xg[0].T
        if it.g == 0:
            for f in range(it.f, it.f + it.n):
                wi_copy(f).wait()
                wo_copy(f).wait()

        def chunk(c0):
            cols = pl.ds(c0, COLS)
            pre = dot(xg[0, pl.ds(it.r0, R)], wi[:, cols])
            mine[it.g, 0, :, cols] = pre[:H]
            csend[it.g, 0, :, cols] = pre[H:].astype(BF16)
            grad = dot_nt(xg[1, pl.ds(it.r0, R)], wo[cols])
            mine[it.g, 1, :, cols] = grad[:H]
            csend[it.g, 1, :, cols] = grad[H:].astype(BF16)

        chunks(it, chunk)
        start(it, "c")

    def chunks(it, run):
        if it.n == 1:
            run(it.c0)
        else:
            @pl.loop(0, it.n)
            def _(j):
                run(pl.multiple_of(it.c0 + j * COLS, COLS))

    def y_first(it, block):
        g, h, bc = it.g, pl.ds(0, it.rows), it.bcols
        b = block(2)
        yp[g, 0, h, bc] = b[0].astype(BF16)
        ym[g, 1, h, bc] = b[1].astype(BF16)
        b = block(1)
        yrel[g, 0, h, bc] = b[0]
        yp[g, 1, h, bc] = b[1].astype(BF16)
        start(it, "y+")
        b = block(3)
        yrel[g, 1, h, bc] = b[1]
        ym[g, 0, h, bc] = b[0].astype(BF16)
        start(it, "y-")
        yown[g, :, h, bc] = block(0)

    def y_relay(it):
        g, h, bc = it.g, pl.ds(0, it.rows), it.bcols
        wait(it, "y+")
        yq[g, 0, h, bc] = (yrel[g, 0, h, bc] + rp[g, 0, h, bc].astype(F32)).astype(BF16)
        start(it, "r+")
        wait(it, "y-")
        yq[g, 1, h, bc] = (yrel[g, 1, h, bc] + rm[g, 1, h, bc].astype(F32)).astype(BF16)
        start(it, "r-")
        yown[g, 0, h, bc] += rm[g, 0, h, bc].astype(F32)
        yown[g, 1, h, bc] += rp[g, 1, h, bc].astype(F32)

    def y_last(it):
        g, h, bc = it.g, pl.ds(0, it.rows), it.bcols
        wait(it, "r+", "r-")
        return yown[g, :, h, bc] + rq[g, :, h, bc].astype(F32)

    def gelu(it, total):
        value, slope = gelu_parts(total[0])
        ag[0, pl.ds(it.r0, Q), it.ycols(0)] = value.astype(BF16)
        ag[1, pl.ds(it.r0, Q), it.ycols(0)] = (total[1] * slope).astype(BF16)

    def even1(it):
        wait(it, "c")
        y_first(it, lambda dy: mine[it.g, :, :, it.ycols(dy)] + crecv[it.g, :, :, it.ycols(dy)].astype(F32))

    def even3(it):
        total = y_last(it)
        zs[it.g, :, :, it.bcols] = total[:, Q:].astype(BF16)
        start(it, "z")
        zmine[it.g, :, :, it.bcols] = total[:, :Q]

    def even4(it):
        wait(it, "z")
        gelu(it, zmine[it.g, :, :, it.bcols] + zr[it.g, :, :, it.bcols].astype(F32))
        start(it, ("Z", 1))

    def even9(it):
        start(it, ("Z", 0))

    def y_gather(it, a):
        wait(it, ("Z", a))
        start(it, ("Y+", a), ("Y-", a))

    def odd1(it):
        g, low, high, c = it.g, pl.ds(0, Q), pl.ds(Q, Q), it.cols
        wait(it, "c")
        zsw[g, :, :, c] = (mine[g, :, high, c] + crecv[g, :, high, c].astype(F32)).astype(BF16)
        start(it, "z")
        mine[g, :, low, c] += crecv[g, :, low, c].astype(F32)

    def odd2(it):
        wait(it, "z")
        y_first(it, lambda dy: mine[it.g, :, pl.ds(0, Q), it.ycols(dy)] + zrw[it.g, :, :, it.ycols(dy)].astype(F32))

    def odd4(it):
        gelu(it, y_last(it))
        start(it, ("Y+", 1), ("Y-", 1))

    def odd9(it):
        start(it, ("Y+", 0), ("Y-", 0))

    def y_forward(it, a):
        wait(it, ("Y+", a))
        start(it, ("R+", a))
        wait(it, ("Y-", a))
        start(it, ("R-", a))

    def even_core(it, a):
        wait(it, ("R+", a), ("R-", a))
        start(it, ("C", a))

    def z_gather(it, a):
        wait(it, ("R+", a), ("R-", a))
        start(it, ("Z", a))

    def odd_core(it, a):
        wait(it, ("Z", a))
        start(it, ("C", a))

    def end(it):
        wait(it, ("C", 0))

    def d_copy(i, g, k):
        return remote(dsend.at[i], drecv.at[i], d_send.at[i], d_recv.at[i], dp_peer(g, k))

    summed = [0] * GROUPS

    def hidden_sum(it):
        wait(it, ("C", 1))

        def chunk(c0):
            cols = pl.ds(c0, COLS)
            acc[pl.ds(it.r0, R)] += dot_nt(ag[1, pl.ds(it.r0, R), cols], wi[:, cols])

        chunks(it, chunk)
        summed[it.g] += it.n
        if summed[it.g] == NF:
            for i, (g, k) in enumerate(dps):
                if g == it.g:
                    rows = pl.multiple_of(g * R + slot_of(rem(x + k, NX)) * T, T)
                    dsend[i] = acc[pl.ds(rows, T)].astype(BF16)
                    d_copy(i, g, k).start()

    def grad_w_in(it):
        def chunk(c0):
            cols = pl.ds(c0, COLS)
            gwi_ref[:, cols] = (dot(xt[...], ag[1, :, cols]) * FACTOR).astype(BF16)

        chunks(it, chunk)

    def grad_w_out(it):
        def chunk(c0):
            cols = pl.ds(c0, COLS)
            gwo_ref[cols, :] = (dot_tn(ag[0, :, cols], xg[1]) * FACTOR).astype(BF16)

        chunks(it, chunk)

    acc[...] = jnp.zeros_like(acc)

    def of(stage, a):
        return lambda it: stage(it, a)

    tail = (end, grad_w_in, grad_w_out)
    stages = (
        (products, even1, y_relay, even3, even4, of(y_gather, 1), of(y_forward, 1), of(even_core, 1), hidden_sum)
        + (even9, of(y_gather, 0), of(y_forward, 0), of(even_core, 0)) + tail,
        (products, odd1, odd2, y_relay, odd4, of(y_forward, 1), of(z_gather, 1), of(odd_core, 1), hidden_sum)
        + (odd9, of(y_forward, 0), of(z_gather, 0), of(odd_core, 0)) + tail,
    )
    items = [Item(i) for i in range(len(ITEMS))]
    for i, n in ORDER:
        stages[items[i].odd][n](items[i])

    total = acc[pl.ds(own, T)]
    for i, (g, k) in enumerate(dps):
        d_copy(i, g, k).wait_recv()
        total = total + drecv[i].astype(F32)
    in_ref[...] = total

    for i, (g, k) in enumerate(dps):
        a_copy(i, g, k)[0].wait_send()
        d_copy(i, g, k).wait_send()
    for it in items:
        for name in NAMES:
            src, dst, _, send, recv, peer = item_copy(it, name)
            remote(src, dst, send, recv, peer).wait_send()


def store_kernel(done, in_ref, gwi_ref, gwo_ref, xg, ag, in_out, gwi_out, gwo_out, gwo, sem):
    head = pl.ds(0, done)
    copies = [
        pltpu.make_async_copy(gwo_ref, gwo_out.at[head], sem.at[2]),
        pltpu.make_async_copy(gwi_ref, gwi_out, sem.at[1]),
        pltpu.make_async_copy(in_ref, in_out, sem.at[0]),
    ]
    for c in copies:
        c.start()
    for i, c0 in enumerate(range(done, ag.shape[2], COLS)):
        cols = pl.ds(c0, COLS)
        gwo[i] = (dot_tn(ag[0, :, cols], xg[1]) * FACTOR).astype(BF16)
        copies.append(pltpu.make_async_copy(gwo.at[i], gwo_out.at[cols], sem.at[3 + i]))
        copies[-1].start()
    for c in copies:
        c.wait()


def local(inputs, out_grads, w_in, w_out):
    T, D = inputs.shape
    FF = w_in.shape[1]
    NF = FF // COLS
    R = NX * T
    H, Q, TOK, BF = R // 2, R // 4, GROUPS * R, FF // NY
    DPS = GROUPS * NX - 1
    done = FF - STORED_LATE * COLS
    vmem = pl.BlockSpec(memory_space=pltpu.VMEM)
    hbm = pl.BlockSpec(memory_space=pl.ANY)
    dma = pltpu.SemaphoreType.DMA
    G = GROUPS
    parts = pl.pallas_call(
        functools.partial(block_kernel, T, D, NF),
        out_shape=[
            pltpu.VMEM((T, D), F32),
            pltpu.VMEM((D, FF), BF16),
            pltpu.VMEM((done, D), BF16),
            pltpu.VMEM((2, TOK, D), BF16),
            pltpu.VMEM((2, TOK, FF), BF16),
        ],
        in_specs=[hbm] * 4,
        out_specs=[vmem] * 5,
        scratch_shapes=[
            pltpu.VMEM((D, TOK), BF16),
            pltpu.VMEM((D, FF), BF16),
            pltpu.VMEM((FF, D), BF16),
            pltpu.VMEM((TOK, D), F32),
            pltpu.VMEM((G, 2, H, FF), BF16),
            pltpu.VMEM((G, 2, H, FF), BF16),
            pltpu.VMEM((G, 2, H, FF), F32),
            *[pltpu.VMEM((G, 2, H, BF), BF16)] * 6,
            *[pltpu.VMEM((G, 2, H, BF), F32)] * 2,
            pltpu.VMEM((G, 2, Q, BF), F32),
            *[pltpu.VMEM((G, 2, Q, BF), BF16)] * 2,
            *[pltpu.VMEM((G, 2, Q, FF), BF16)] * 2,
            pltpu.VMEM((DPS, T, D), BF16),
            pltpu.VMEM((DPS, T, D), BF16),
            dma((2,)), dma((NF,)), dma((NF,)),
            dma((DPS,)), dma((DPS,)),
            dma((len(ITEMS), len(NAMES))), dma((len(ITEMS), len(NAMES))),
            dma((DPS,)), dma((DPS,)),
        ],
        compiler_params=pltpu.CompilerParams(
            collective_id=0, has_side_effects=True, vmem_limit_bytes=38 * 2**20
        ),
        name="ffn_backward",
    )(inputs, out_grads, w_in, w_out)
    return pl.pallas_call(
        functools.partial(store_kernel, done),
        out_shape=[
            jax.ShapeDtypeStruct((T, D), F32),
            jax.ShapeDtypeStruct((D, FF), BF16),
            jax.ShapeDtypeStruct((FF, D), BF16),
        ],
        in_specs=[vmem] * 5,
        out_specs=[hbm] * 3,
        scratch_shapes=[
            pltpu.VMEM((max(STORED_LATE, 1), COLS, D), BF16),
            dma((3 + STORED_LATE,)),
        ],
        compiler_params=pltpu.CompilerParams(vmem_limit_bytes=12 * 2**20),
        name="store_results",
    )(*parts)


def solution(mesh):
    return jax.shard_map(
        local,
        mesh=mesh,
        in_specs=(P("dp", "mp"), P("dp", "mp"), P("mp", "dp"), P("dp", "mp")),
        out_specs=(P("dp", "mp"), P("mp", "dp"), P("dp", "mp")),
        check_vma=False,
    )
```

time: 326 us -> 71.6 us (0.22)
  waiting for transfers between devices: 199 us -> 0 us
  blocking collectives: 70.3 us -> 0 us
  Pallas kernels: 0 us -> 69.1 us
  matrix products: 26.3 us -> 0 us
  between operations: 14.1 us -> 0.65 us
  local copies, waits for them, and re-layouts: 10.3 us -> 1.55 us
  other arithmetic: 4.88 us -> 0 us
    psum x1 -> x0, waiting for transfers between devices: 148 us -> none  [local(): preact, grad_act = lax.psum((partial_pre, partial_grad), 'mp')]
    all_gather x2 -> x0, blocking collectives: 70.3 us -> none  [the longest x1 35.3 us: local(): lax.all_gather(inputs, 'dp', axis=0, tiled=True)]
    pallas_call x0 -> x2, Pallas kernels: none -> 69.1 us  [the longest x1 64.6 us: local(): pl.pallas_call(functools.partial(block_kernel, T, D, NF), out_shape=[pltp...]
    reduce_scatter x1 -> x0, waiting for transfers between devices: 50.8 us -> none  [local(): lax.psum_scatter(partial_all, 'dp', scatter_dimension=0, tiled=True)]
    dot_general x5 -> x0, matrix products: 26.3 us -> none  [the longest x2 12.2 us: contract_rows(): lax.dot_general(left, right, (((0,), (0,)), ((), ())), preferred_element_...]
    unnamed x11 -> x4, local copies, waits for them, and re-layouts: 10.3 us -> 1.55 us
    convert_element_type x1 -> x0, other arithmetic: 4.88 us -> none  [finish(): grad_preact = (grad_act * gelu_slope).astype(jnp.bfloat16)]
  transfers between devices with their start and end apart: 2 -> 0, of which waited for: 2 -> 0; matrix products, arithmetic and copies ran while one was open for 6% -> 0% of each run, Pallas kernels for 0% -> 0%
where the time goes in v3:
time: 71.6 us; the launch traced here: 71.3 us
  Pallas kernels  69.1 us (97%)
  local copies, waits for them, and re-layouts  1.55 us (2%)
    pallas_call x1, Pallas kernels, local(): pl.pallas_call(functools.partial(block_kernel, T, D, NF), out_shape=[pltp...  64.6 us
    pallas_call x1, Pallas kernels, local(): pl.pallas_call(functools.partial(store_kernel, done), out_shape=[jax.Shap...  4.54 us
    unnamed x4, local copies, waits for them, and re-layouts  1.55 us

profile of v3, /device:TPU:0, one launch (start us, length us, event | category | flops | bytes accessed | tf_op | source)
XLA Modules:
  0.0 71.3 jit_solution(3896830201335880535)
XLA Ops:
  0.6 0.0 copy-start
  0.6 0.8 %copy-done = bf16[32,640]{1,0:T(8,128)(2,1)S(1)} copy-done((bf16[32,640]{1,0:T(8,128)(2,1)S(1)}, bf16[32,640]{1,0:T(8,128)(2,1)}, u32[]{:S(2)}) %copy-start) | copy-done | bytes 40984
  1.4 0.0 copy-start.1
  1.4 0.8 %copy-done.1 = bf16[32,640]{1,0:T(8,128)(2,1)S(1)} copy-done((bf16[32,640]{1,0:T(8,128)(2,1)S(1)}, bf16[32,640]{1,0:T(8,128)(2,1)}, u32[]{:S(2)}) %copy-start.1) | copy-done | bytes 40984
  2.2 64.6 %ffn_backward.1 = (f32[32,640]{1,0:T(8,128)S(1)}, bf16[640,4608]{1,0:T(8,128)(2,1)S(1)}, bf16[2560,640]{1,0:T(8,128)(2,1)S(1)}, bf16[2,256,640]{2,1,0:T(8,128)(2,1)S(1)}, bf16[2,256,4608]{2,1,0:T(8,128)(2,1)S(1)}) custom-call(bf16[32,640]{1,0:T(8,128)(2,1)S(1)} %copy-done, bf16[32,640]{1,0:T(8,128)(2,1)S(1)} %copy-done.1, bf16[640,4608]{1,0:T(8,128)(2,1)} %wi_hbm.1, ...), custom_call_target="tpu_custom_call" | custom-call | tf_op jit(solution)/shard_map/ffn_backward/pallas_call | solution.py:447
  66.8 4.5 %store_results.1 = (f32[32,640]{1,0:T(8,128)}, bf16[640,4608]{1,0:T(8,128)(2,1)}, bf16[4608,640]{1,0:T(8,128)(2,1)}) custom-call(f32[32,640]{1,0:T(8,128)S(1)} %get-tuple-element.8.in_ref, bf16[640,4608]{1,0:T(8,128)(2,1)S(1)} %get-tuple-element.9.gwi_ref, bf16[2560,640]{1,0:T(8,128)(2,1)S(1)} %get-tuple-element.10.gwo_ref, ...), custom_call_target="tpu_custom_call" | custom-call | tf_op jit(solution)/shard_map/store_results/pallas_call | solution.py:483
Async XLA Ops:
  0.6 0.8 %copy-start = (bf16[32,640]{1,0:T(8,128)(2,1)S(1)}, bf16[32,640]{1,0:T(8,128)(2,1)}, u32[]{:S(2)}) copy-start(bf16[32,640]{1,0:T(8,128)(2,1)} %x_hbm.1) | copy-start | bytes 122884
  1.4 0.8 %copy-start.1 = (bf16[32,640]{1,0:T(8,128)(2,1)S(1)}, bf16[32,640]{1,0:T(8,128)(2,1)}, u32[]{:S(2)}) copy-start(bf16[32,640]{1,0:T(8,128)(2,1)} %g_hbm.1) | copy-start | bytes 122884

commit v4 on v3

--- a/solution.py
+++ b/solution.py
@@ -13,32 +13,38 @@
 
 NX, NY = 4, 4
 FACTOR = 1.0 / math.sqrt(256)
-GROUPS = 2
+PLACES = (((0, 0), (1, 0), (3, 0), (0, 1)), ((2, 0), (1, 1), (3, 1), (2, 1)))
+GROUPS = len(PLACES)
 COLS = 512
 ITEMS = (
-    (0, 0, 3, 1),
-    (0, 3, 3, 0),
-    (0, 6, 3, 0),
+    (0, 0, 2, 1),
+    (0, 2, 3, 0),
+    (0, 5, 2, 1),
+    (0, 7, 2, 0),
     (1, 0, 2, 1),
-    (1, 2, 3, 0),
-    (1, 5, 2, 1),
-    (1, 7, 2, 0),
+    (1, 2, 2, 1),
+    (1, 4, 2, 0),
+    (1, 6, 2, 0),
+    (1, 8, 1, 1),
 )
 ORDER = (
-    (0, 0), (1, 0), (0, 1), (2, 0), (1, 1), (3, 0), (2, 1), (4, 0), (3, 1), (1, 2),
-    (0, 2), (5, 0), (4, 1), (2, 2), (6, 0), (5, 1), (3, 2), (1, 3), (0, 3), (6, 1),
-    (4, 2), (2, 3), (3, 3), (0, 4), (0, 9), (5, 2), (6, 2), (1, 4), (1, 9), (4, 3),
-    (2, 4), (3, 4), (0, 5), (3, 9), (2, 9), (0, 10), (5, 3), (1, 5), (1, 10), (6, 3),
-    (3, 5), (0, 6), (4, 4), (4, 9), (3, 10), (2, 5), (0, 11), (5, 4), (5, 9), (2, 10),
-    (6, 4), (1, 6), (6, 9), (1, 11), (3, 6), (3, 11), (0, 7), (2, 6), (4, 5), (5, 5),
-    (4, 10), (5, 10), (0, 8), (2, 11), (1, 7), (0, 12), (1, 12), (6, 5), (2, 7), (6, 10),
-    (1, 8), (5, 6), (4, 6), (1, 13), (0, 13), (3, 7), (2, 8), (5, 11), (4, 11), (3, 8),
-    (3, 12), (2, 12), (6, 6), (3, 14), (6, 11), (5, 7), (4, 7), (3, 13), (2, 13), (3, 15),
-    (6, 7), (5, 8), (4, 8), (6, 12), (5, 12), (6, 8), (4, 12), (4, 14), (6, 13), (5, 13),
-    (5, 14), (4, 13), (6, 14), (4, 15),
+    (0, 0), (1, 0), (0, 1), (2, 0), (1, 1), (3, 0), (2, 1), (4, 0), (3, 1), (0, 2),
+    (5, 0), (4, 1), (1, 2), (6, 0), (5, 1), (3, 2), (2, 2), (0, 3), (7, 0), (6, 1),
+    (1, 3), (8, 0), (4, 2), (7, 1), (3, 3), (2, 3), (0, 4), (8, 1), (5, 2), (6, 2),
+    (1, 4), (4, 3), (3, 4), (0, 9), (7, 2), (2, 4), (8, 2), (0, 5), (5, 3), (1, 5),
+    (6, 3), (3, 5), (4, 4), (1, 9), (0, 10), (7, 3), (2, 5), (8, 3), (0, 6), (5, 4),
+    (2, 9), (6, 4), (3, 9), (1, 10), (1, 6), (3, 6), (7, 4), (4, 5), (4, 9), (2, 6),
+    (8, 4), (8, 9), (5, 5), (7, 9), (6, 9), (0, 7), (5, 9), (2, 10), (6, 5), (0, 11),
+    (3, 10), (1, 11), (7, 5), (1, 7), (0, 8), (4, 6), (3, 7), (4, 10), (8, 5), (8, 10),
+    (2, 7), (5, 6), (7, 10), (5, 10), (2, 11), (6, 10), (1, 8), (6, 6), (2, 8), (3, 11),
+    (0, 12), (1, 12), (3, 8), (7, 6), (8, 6), (4, 7), (8, 11), (4, 11), (0, 13), (7, 11),
+    (1, 13), (5, 11), (5, 7), (6, 11), (4, 8), (6, 7), (3, 12), (4, 14), (7, 7), (2, 12),
+    (8, 7), (7, 12), (5, 8), (8, 12), (3, 13), (6, 12), (6, 8), (7, 8), (2, 13), (8, 8),
+    (8, 13), (7, 13), (6, 13), (4, 12), (5, 14), (5, 12), (6, 14), (4, 13), (7, 14), (5, 13),
+    (8, 14), (4, 15), (5, 15), (6, 15),
 )
-STORED_LATE = 4
-SUMS = ("c", "y+", "y-", "r+", "r-", "z")
+STORED_LATE = 3
+SUMS = ("y+", "y-", "r+", "r-", "z")
 GATHERS = tuple((name, a) for a in range(2) for name in ("Z", "Y+", "Y-", "R+", "R-", "C"))
 NAMES = SUMS + GATHERS
 
@@ -49,10 +55,6 @@
 
 def div(a, b):
     return lax.div(a, jnp.int32(b))
-
-
-def mult(v, m):
-    return pl.multiple_of(v * m, m)
 
 
 def dot(a, b):
@@ -79,7 +81,7 @@
     in_ref, gwi_ref, gwo_ref, xg, ag,
     xt, wi, wo, acc,
     csend, crecv, mine, yp, ym, yq, rp, rm, rq, yown, yrel, zmine, zs, zr, zsw, zrw, dsend, drecv,
-    load_sem, wi_sem, wo_sem, a_send, a_recv, i_send, i_recv, d_send, d_recv,
+    load_sem, wi_sem, wo_sem, a_send, a_recv, c_send, c_recv, i_send, i_recv, d_send, d_recv,
 ):
     R = NX * T
     H, Q = R // 2, R // 4
@@ -87,25 +89,31 @@
     x, zhi = div(dp, 2), rem(dp, 2)
     zlo, y, core = div(mp, 8), rem(div(mp, 2), NY), rem(mp, 2)
 
-    def slot_of(j):
-        return rem(div(j, 2) + core, 2) * 2 + rem(rem(j, 2) + zlo, 2)
+    def rows_of(g, j):
+        slot = rem(j // 2 + core, 2) * 2 + rem(j % 2 + zlo, 2)
+        return pl.ds(pl.multiple_of(g * R + slot * T, T), T)
+
+    def rows_from(dx, dz):
+        for g, places in enumerate(PLACES):
+            if (dx, dz) in places:
+                return rows_of(g, places.index((dx, dz)))
 
     def mp_peer(dz=0, dy=0, dc=0):
         return (dp, rem(zlo + dz, 2) * 8 + rem(y + dy, NY) * 2 + rem(core + dc, 2))
 
-    def dp_peer(g, k):
-        return (rem(x + k, NX) * 2 + rem(zhi + g, 2), mp)
+    def dp_peer(dx, dz):
+        return (rem(x + dx, NX) * 2 + rem(zhi + dz, 2), mp)
 
     peers = [mp_peer(dc=1), mp_peer(dz=1)] + [mp_peer(dy=k) for k in range(1, NY)]
-    dps = [(g, k) for g in range(GROUPS) for k in range(NX) if g or k]
+    dps = [place for places in PLACES for place in places if place != (0, 0)]
     barrier = pltpu.get_barrier_semaphore()
-    for peer in peers + [dp_peer(g, k) for g, k in dps]:
+    for peer in peers + [dp_peer(*place) for place in dps]:
         pl.semaphore_signal(barrier, inc=1, device_id=peer, device_id_type=MESH)
 
-    own = mult(slot_of(x), T)
+    own = rows_of(0, 0)
     loads = [
-        pltpu.make_async_copy(x_hbm, xg.at[0, pl.ds(own, T)], load_sem.at[0]),
-        pltpu.make_async_copy(g_hbm, xg.at[1, pl.ds(own, T)], load_sem.at[1]),
+        pltpu.make_async_copy(x_hbm, xg.at[0, own], load_sem.at[0]),
+        pltpu.make_async_copy(g_hbm, xg.at[1, own], load_sem.at[1]),
     ]
     for c in loads:
         c.start()
@@ -127,28 +135,30 @@
             src_ref=src, dst_ref=dst, send_sem=send, recv_sem=recv, device_id=peer, device_id_type=MESH
         )
 
-    def a_copy(i, g, k):
-        src = xg.at[:, pl.ds(pl.multiple_of((R if k and g else 0) + own, T), T)]
-        dst = xg.at[:, pl.ds(pl.multiple_of(g * R + own, T), T)]
-        land = xg.at[:, pl.ds(pl.multiple_of(g * R + slot_of(rem(x + NX - k, NX)) * T, T), T)]
-        peer = dp_peer(0, k) if k else dp_peer(g, 0)
-        return remote(src, dst, a_send.at[i], a_recv.at[i], peer), remote(land, land, a_send.at[i], a_recv.at[i], peer)
-
-    def gather_start(pick):
-        for i, (g, k) in enumerate(dps):
-            if pick(g, k):
-                a_copy(i, g, k)[0].start()
-
-    def gather_wait(pick):
-        for i, (g, k) in enumerate(dps):
-            if pick(g, k):
-                a_copy(i, g, k)[1].wait_recv()
+    def a_copy(i):
+        dx, dz = dps[i]
+        back = (-dx) % NX
+        src = rows_from(0, 1) if dx and dz else own
+        peer = dp_peer(dx, 0) if dx else dp_peer(0, dz)
+        rows = rows_from(back, dz)
+        send = remote(xg.at[:, src], xg.at[:, rows], a_send.at[i], a_recv.at[i], peer)
+        return send, remote(xg.at[:, rows], xg.at[:, rows], a_send.at[i], a_recv.at[i], peer)
+
+    def gather_start(*places):
+        for place in places:
+            a_copy(dps.index(place))[0].start()
+
+    def gather_wait(*places):
+        for place in places:
+            a_copy(dps.index(place))[1].wait_recv()
+
+    near, partner = ((1, 0), (3, 0)), (0, 1)
+    opposite, beyond = (2, 0), ((1, 1), (3, 1), (2, 1))
 
     for c in loads:
         c.wait()
     pl.semaphore_wait(barrier, len(peers) + len(dps))
-    gather_start(lambda g, k: g == 0)
-    gather_start(lambda g, k: k == 0)
+    gather_start(*near, partner)
 
     class Item:
         def __init__(self, i):
@@ -169,9 +179,7 @@
         up, down, zp, cp = mp_peer(dy=1), mp_peer(dy=NY - 1), mp_peer(dz=1), mp_peer(dc=1)
         head, own_z, other_z, gather = pl.ds(0, it.rows), pl.ds(r0, Q), pl.ds(r0 + Q, Q), pl.ds(r0, it.rows)
         land = None
-        if name == "c":
-            src, dst, peer = csend.at[g, :, :, it.cols], crecv.at[g, :, :, it.cols], cp
-        elif name == "y+":
+        if name == "y+":
             src, dst, peer = yp.at[g, :, head, bc], rp.at[g, :, head, bc], up
         elif name == "y-":
             src, dst, peer = ym.at[g, :, head, bc], rm.at[g, :, head, bc], down
@@ -217,14 +225,20 @@
             _, _, land, send, recv, peer = item_copy(it, name)
             remote(land, land, send, recv, peer).wait_recv()
 
+    def core_copy(g, c0):
+        cols, n = pl.ds(c0, COLS), g * NF + c0 // COLS
+        return remote(csend.at[g, :, :, cols], crecv.at[g, :, :, cols], c_send.at[n], c_recv.at[n], mp_peer(dc=1))
+
+    def core_wait(it):
+        for f in range(it.f, it.f + it.n):
+            core_copy(it.g, f * COLS).wait_recv()
+
     def products(it):
         if it.i == 0:
-            gather_wait(lambda g, k: g == 0)
-        if it.i == 1:
-            gather_wait(lambda g, k: k == 0)
-            gather_start(lambda g, k: g and k)
+            gather_wait(*near, partner)
+            gather_start(opposite, *beyond)
         if it.g == 1 and it.f == 0:
-            gather_wait(lambda g, k: g and k)
+            gather_wait(opposite, *beyond)
             xt[...] = xg[0].T
         if it.g == 0:
             for f in range(it.f, it.f + it.n):
@@ -239,9 +253,9 @@
             grad = dot_nt(xg[1, pl.ds(it.r0, R)], wo[cols])
             mine[it.g, 1, :, cols] = grad[:H]
             csend[it.g, 1, :, cols] = grad[H:].astype(BF16)
+            core_copy(it.g, c0).start()
 
         chunks(it, chunk)
-        start(it, "c")
 
     def chunks(it, run):
         if it.n == 1:
@@ -288,7 +302,7 @@
         ag[1, pl.ds(it.r0, Q), it.ycols(0)] = (total[1] * slope).astype(BF16)
 
     def even1(it):
-        wait(it, "c")
+        core_wait(it)
         y_first(it, lambda dy: mine[it.g, :, :, it.ycols(dy)] + crecv[it.g, :, :, it.ycols(dy)].astype(F32))
 
     def even3(it):
@@ -311,7 +325,7 @@
 
     def odd1(it):
         g, low, high, c = it.g, pl.ds(0, Q), pl.ds(Q, Q), it.cols
-        wait(it, "c")
+        core_wait(it)
         zsw[g, :, :, c] = (mine[g, :, high, c] + crecv[g, :, high, c].astype(F32)).astype(BF16)
         start(it, "z")
         mine[g, :, low, c] += crecv[g, :, low, c].astype(F32)
@@ -345,11 +359,19 @@
         wait(it, ("Z", a))
         start(it, ("C", a))
 
+    def sent(it, names):
+        for name in names:
+            src, dst, _, send, recv, peer = item_copy(it, name)
+            remote(src, dst, send, recv, peer).wait_send()
+
     def end(it):
         wait(it, ("C", 0))
-
-    def d_copy(i, g, k):
-        return remote(dsend.at[i], drecv.at[i], d_send.at[i], d_recv.at[i], dp_peer(g, k))
+        sent(it, [name for name in NAMES if name in SUMS or name[1] == 1])
+        for f in range(it.f, it.f + it.n):
+            core_copy(it.g, f * COLS).wait_send()
+
+    def d_copy(i):
+        return remote(dsend.at[i], drecv.at[i], d_send.at[i], d_recv.at[i], dp_peer(*dps[i]))
 
     summed = [0] * GROUPS
 
@@ -363,11 +385,10 @@
         chunks(it, chunk)
         summed[it.g] += it.n
         if summed[it.g] == NF:
-            for i, (g, k) in enumerate(dps):
-                if g == it.g:
-                    rows = pl.multiple_of(g * R + slot_of(rem(x + k, NX)) * T, T)
-                    dsend[i] = acc[pl.ds(rows, T)].astype(BF16)
-                    d_copy(i, g, k).start()
+            for i, place in enumerate(dps):
+                if place in PLACES[it.g]:
+                    dsend[i] = acc[rows_from(*place)].astype(BF16)
+                    d_copy(i).start()
 
     def grad_w_in(it):
         def chunk(c0):
@@ -399,19 +420,17 @@
     for i, n in ORDER:
         stages[items[i].odd][n](items[i])
 
-    total = acc[pl.ds(own, T)]
-    for i, (g, k) in enumerate(dps):
-        d_copy(i, g, k).wait_recv()
+    total = acc[own]
+    for i in range(len(dps)):
+        d_copy(i).wait_recv()
         total = total + drecv[i].astype(F32)
     in_ref[...] = total
 
-    for i, (g, k) in enumerate(dps):
-        a_copy(i, g, k)[0].wait_send()
-        d_copy(i, g, k).wait_send()
+    for i in range(len(dps)):
+        a_copy(i)[0].wait_send()
+        d_copy(i).wait_send()
     for it in items:
-        for name in NAMES:
-            src, dst, _, send, recv, peer = item_copy(it, name)
-            remote(src, dst, send, recv, peer).wait_send()
+        sent(it, [name for name in GATHERS if name[1] == 0])
 
 
 def store_kernel(done, in_ref, gwi_ref, gwo_ref, xg, ag, in_out, gwi_out, gwo_out, gwo, sem):
@@ -441,7 +460,7 @@
     DPS = GROUPS * NX - 1
     done = FF - STORED_LATE * COLS
     vmem = pl.BlockSpec(memory_space=pltpu.VMEM)
-    hbm = pl.BlockSpec(memory_space=pl.ANY)
+    hbm = pl.BlockSpec(memory_space=pltpu.HBM)
     dma = pltpu.SemaphoreType.DMA
     G = GROUPS
     parts = pl.pallas_call(
@@ -472,11 +491,12 @@
             pltpu.VMEM((DPS, T, D), BF16),
             dma((2,)), dma((NF,)), dma((NF,)),
             dma((DPS,)), dma((DPS,)),
+            dma((G * NF,)), dma((G * NF,)),
             dma((len(ITEMS), len(NAMES))), dma((len(ITEMS), len(NAMES))),
             dma((DPS,)), dma((DPS,)),
         ],
         compiler_params=pltpu.CompilerParams(
-            collective_id=0, has_side_effects=True, vmem_limit_bytes=38 * 2**20
+            collective_id=0, has_side_effects=True, vmem_limit_bytes=44 * 2**20
         ),
         name="ffn_backward",
     )(inputs, out_grads, w_in, w_out)

time: 71.6 us -> 69.8 us (0.975)
  local copies, waits for them, and re-layouts: 1.55 us -> 0 us
    unnamed x4 -> x0, local copies, waits for them, and re-layouts: 1.55 us -> none
where the time goes in v4:
time: 69.8 us; the launch traced here: 69.7 us
  Pallas kernels  69.1 us (99%)
    pallas_call x1, Pallas kernels, local(): pl.pallas_call(functools.partial(block_kernel, T, D, NF), out_shape=[pltp...  64.5 us
    pallas_call x1, Pallas kernels, local(): pl.pallas_call(functools.partial(store_kernel, done), out_shape=[jax.Shap...  4.56 us

profile of v4, /device:TPU:0, one launch (start us, length us, event | category | flops | bytes accessed | tf_op | source)
XLA Modules:
  0.0 69.7 jit_solution(6019891735382241623)
XLA Ops:
  0.6 64.5 %ffn_backward.1 = (f32[32,640]{1,0:T(8,128)S(1)}, bf16[640,4608]{1,0:T(8,128)(2,1)S(1)}, bf16[3072,640]{1,0:T(8,128)(2,1)S(1)}, bf16[2,256,640]{2,1,0:T(8,128)(2,1)S(1)}, bf16[2,256,4608]{2,1,0:T(8,128)(2,1)S(1)}) custom-call(bf16[32,640]{1,0:T(8,128)(2,1)} %x_hbm.1, bf16[32,640]{1,0:T(8,128)(2,1)} %g_hbm.1, bf16[640,4608]{1,0:T(8,128)(2,1)} %wi_hbm.1, ...), custom_call_target="tpu_custom_call" | custom-call | tf_op jit(solution)/shard_map/ffn_backward/pallas_call | solution.py:466
  65.1 4.6 %store_results.1 = (f32[32,640]{1,0:T(8,128)}, bf16[640,4608]{1,0:T(8,128)(2,1)}, bf16[4608,640]{1,0:T(8,128)(2,1)}) custom-call(f32[32,640]{1,0:T(8,128)S(1)} %get-tuple-element.8.in_ref, bf16[640,4608]{1,0:T(8,128)(2,1)S(1)} %get-tuple-element.9.gwi_ref, bf16[3072,640]{1,0:T(8,128)(2,1)S(1)} %get-tuple-element.10.gwo_ref, ...), custom_call_target="tpu_custom_call" | custom-call | tf_op jit(solution)/shard_map/store_results/pallas_call | solution.py:503

commit v5 on v4

--- a/solution.py
+++ b/solution.py
@@ -41,9 +41,9 @@
     (1, 13), (5, 11), (5, 7), (6, 11), (4, 8), (6, 7), (3, 12), (4, 14), (7, 7), (2, 12),
     (8, 7), (7, 12), (5, 8), (8, 12), (3, 13), (6, 12), (6, 8), (7, 8), (2, 13), (8, 8),
     (8, 13), (7, 13), (6, 13), (4, 12), (5, 14), (5, 12), (6, 14), (4, 13), (7, 14), (5, 13),
-    (8, 14), (4, 15), (5, 15), (6, 15),
+    (8, 14), (4, 15), (5, 15),
 )
-STORED_LATE = 3
+STORED_LATE = 5
 SUMS = ("y+", "y-", "r+", "r-", "z")
 GATHERS = tuple((name, a) for a in range(2) for name in ("Z", "Y+", "Y-", "R+", "R-", "C"))
 NAMES = SUMS + GATHERS
@@ -135,22 +135,23 @@
             src_ref=src, dst_ref=dst, send_sem=send, recv_sem=recv, device_id=peer, device_id_type=MESH
         )
 
-    def a_copy(i):
+    def a_copy(i, a):
         dx, dz = dps[i]
         back = (-dx) % NX
         src = rows_from(0, 1) if dx and dz else own
         peer = dp_peer(dx, 0) if dx else dp_peer(0, dz)
         rows = rows_from(back, dz)
-        send = remote(xg.at[:, src], xg.at[:, rows], a_send.at[i], a_recv.at[i], peer)
-        return send, remote(xg.at[:, rows], xg.at[:, rows], a_send.at[i], a_recv.at[i], peer)
+        sems = a_send.at[i, a], a_recv.at[i, a]
+        return remote(xg.at[a, src], xg.at[a, rows], *sems, peer), remote(xg.at[a, rows], xg.at[a, rows], *sems, peer)
 
     def gather_start(*places):
+        for a in range(2):
+            for place in places:
+                a_copy(dps.index(place), a)[0].start()
+
+    def gather_wait(a, *places):
         for place in places:
-            a_copy(dps.index(place))[0].start()
-
-    def gather_wait(*places):
-        for place in places:
-            a_copy(dps.index(place))[1].wait_recv()
+            a_copy(dps.index(place), a)[1].wait_recv()
 
     near, partner = ((1, 0), (3, 0)), (0, 1)
     opposite, beyond = (2, 0), ((1, 1), (3, 1), (2, 1))
@@ -235,27 +236,40 @@
 
     def products(it):
         if it.i == 0:
-            gather_wait(*near, partner)
-            gather_start(opposite, *beyond)
+            gather_wait(0, *near, partner)
         if it.g == 1 and it.f == 0:
-            gather_wait(opposite, *beyond)
+            gather_wait(0, opposite, *beyond)
+            gather_wait(1, opposite, *beyond)
             xt[...] = xg[0].T
         if it.g == 0:
             for f in range(it.f, it.f + it.n):
                 wi_copy(f).wait()
                 wo_copy(f).wait()
 
-        def chunk(c0):
+        def pre_chunk(c0):
             cols = pl.ds(c0, COLS)
             pre = dot(xg[0, pl.ds(it.r0, R)], wi[:, cols])
             mine[it.g, 0, :, cols] = pre[:H]
             csend[it.g, 0, :, cols] = pre[H:].astype(BF16)
+
+        def grad_chunk(c0):
+            cols = pl.ds(c0, COLS)
             grad = dot_nt(xg[1, pl.ds(it.r0, R)], wo[cols])
             mine[it.g, 1, :, cols] = grad[:H]
             csend[it.g, 1, :, cols] = grad[H:].astype(BF16)
             core_copy(it.g, c0).start()
 
-        chunks(it, chunk)
+        def chunk(c0):
+            pre_chunk(c0)
+            grad_chunk(c0)
+
+        if it.i == 0:
+            chunks(it, pre_chunk)
+            gather_wait(1, *near, partner)
+            gather_start(opposite, *beyond)
+            chunks(it, grad_chunk)
+        else:
+            chunks(it, chunk)
 
     def chunks(it, run):
         if it.n == 1:
@@ -427,7 +441,8 @@
     in_ref[...] = total
 
     for i in range(len(dps)):
-        a_copy(i)[0].wait_send()
+        a_copy(i, 0)[0].wait_send()
+        a_copy(i, 1)[0].wait_send()
         d_copy(i).wait_send()
     for it in items:
         sent(it, [name for name in GATHERS if name[1] == 0])
@@ -490,7 +505,7 @@
             pltpu.VMEM((DPS, T, D), BF16),
             pltpu.VMEM((DPS, T, D), BF16),
             dma((2,)), dma((NF,)), dma((NF,)),
-            dma((DPS,)), dma((DPS,)),
+            dma((DPS, 2)), dma((DPS, 2)),
             dma((G * NF,)), dma((G * NF,)),
             dma((len(ITEMS), len(NAMES))), dma((len(ITEMS), len(NAMES))),
             dma((DPS,)), dma((DPS,)),

time: 69.8 us -> 70 us (level)
  no operation moved by 1% of the time
where the time goes in v5:
time: 70 us; the launch traced here: 69.9 us
  Pallas kernels  69.2 us (99%)
    pallas_call x1, Pallas kernels, local(): pl.pallas_call(functools.partial(block_kernel, T, D, NF), out_shape=[pltp...  64.7 us
    pallas_call x1, Pallas kernels, local(): pl.pallas_call(functools.partial(store_kernel, done), out_shape=[jax.Shap...  4.54 us

profile of v5, /device:TPU:0, one launch (start us, length us, event | category | flops | bytes accessed | tf_op | source)
XLA Modules:
  0.0 69.9 jit_solution(17988709325833802062)
XLA Ops:
  0.6 64.7 %ffn_backward.1 = (f32[32,640]{1,0:T(8,128)S(1)}, bf16[640,4608]{1,0:T(8,128)(2,1)S(1)}, bf16[2048,640]{1,0:T(8,128)(2,1)S(1)}, bf16[2,256,640]{2,1,0:T(8,128)(2,1)S(1)}, bf16[2,256,4608]{2,1,0:T(8,128)(2,1)S(1)}) custom-call(bf16[32,640]{1,0:T(8,128)(2,1)} %x_hbm.1, bf16[32,640]{1,0:T(8,128)(2,1)} %g_hbm.1, bf16[640,4608]{1,0:T(8,128)(2,1)} %wi_hbm.1, ...), custom_call_target="tpu_custom_call" | custom-call | tf_op jit(solution)/shard_map/ffn_backward/pallas_call | solution.py:481
  65.3 4.5 %store_results.1 = (f32[32,640]{1,0:T(8,128)}, bf16[640,4608]{1,0:T(8,128)(2,1)}, bf16[4608,640]{1,0:T(8,128)(2,1)}) custom-call(f32[32,640]{1,0:T(8,128)S(1)} %get-tuple-element.8.in_ref, bf16[640,4608]{1,0:T(8,128)(2,1)S(1)} %get-tuple-element.9.gwi_ref, bf16[2048,640]{1,0:T(8,128)(2,1)S(1)} %get-tuple-element.10.gwo_ref, ...), custom_call_target="tpu_custom_call" | custom-call | tf_op jit(solution)/shard_map/store_results/pallas_call | solution.py:518

commit v6 on v5

--- a/solution.py
+++ b/solution.py
@@ -104,10 +104,12 @@
     def dp_peer(dx, dz):
         return (rem(x + dx, NX) * 2 + rem(zhi + dz, 2), mp)
 
-    peers = [mp_peer(dc=1), mp_peer(dz=1)] + [mp_peer(dy=k) for k in range(1, NY)]
     dps = [place for places in PLACES for place in places if place != (0, 0)]
+    near, partner = ((1, 0), (3, 0)), (0, 1)
+    opposite, beyond = (2, 0), ((1, 1), (3, 1), (2, 1))
+    peers = [mp_peer(dc=1), mp_peer(dz=1), mp_peer(dy=1), mp_peer(dy=NY - 1)] + [dp_peer(*p) for p in (*near, partner)]
     barrier = pltpu.get_barrier_semaphore()
-    for peer in peers + [dp_peer(*place) for place in dps]:
+    for peer in peers:
         pl.semaphore_signal(barrier, inc=1, device_id=peer, device_id_type=MESH)
 
     own = rows_of(0, 0)
@@ -153,12 +155,9 @@
         for place in places:
             a_copy(dps.index(place), a)[1].wait_recv()
 
-    near, partner = ((1, 0), (3, 0)), (0, 1)
-    opposite, beyond = (2, 0), ((1, 1), (3, 1), (2, 1))
-
     for c in loads:
         c.wait()
-    pl.semaphore_wait(barrier, len(peers) + len(dps))
+    pl.semaphore_wait(barrier, len(peers))
     gather_start(*near, partner)
 
     class Item:

time: 70 us -> 69.5 us (level)
  no operation moved by 1% of the time
where the time goes in v6:
time: 69.5 us; the launch traced here: 69.4 us
  Pallas kernels  68.7 us (99%)
    pallas_call x1, Pallas kernels, local(): pl.pallas_call(functools.partial(block_kernel, T, D, NF), out_shape=[pltp...  64.2 us
    pallas_call x1, Pallas kernels, local(): pl.pallas_call(functools.partial(store_kernel, done), out_shape=[jax.Shap...  4.54 us

profile of v6, /device:TPU:0, one launch (start us, length us, event | category | flops | bytes accessed | tf_op | source)
XLA Modules:
  0.0 69.4 jit_solution(2283184364388953387)
XLA Ops:
  0.6 64.2 %ffn_backward.1 = (f32[32,640]{1,0:T(8,128)S(1)}, bf16[640,4608]{1,0:T(8,128)(2,1)S(1)}, bf16[2048,640]{1,0:T(8,128)(2,1)S(1)}, bf16[2,256,640]{2,1,0:T(8,128)(2,1)S(1)}, bf16[2,256,4608]{2,1,0:T(8,128)(2,1)S(1)}) custom-call(bf16[32,640]{1,0:T(8,128)(2,1)} %x_hbm.1, bf16[32,640]{1,0:T(8,128)(2,1)} %g_hbm.1, bf16[640,4608]{1,0:T(8,128)(2,1)} %wi_hbm.1, ...), custom_call_target="tpu_custom_call" | custom-call | tf_op jit(solution)/shard_map/ffn_backward/pallas_call | solution.py:480
  64.8 4.5 %store_results.1 = (f32[32,640]{1,0:T(8,128)}, bf16[640,4608]{1,0:T(8,128)(2,1)}, bf16[4608,640]{1,0:T(8,128)(2,1)}) custom-call(f32[32,640]{1,0:T(8,128)S(1)} %get-tuple-element.8.in_ref, bf16[640,4608]{1,0:T(8,128)(2,1)S(1)} %get-tuple-element.9.gwi_ref, bf16[2048,640]{1,0:T(8,128)(2,1)S(1)} %get-tuple-element.10.gwo_ref, ...), custom_call_target="tpu_custom_call" | custom-call | tf_op jit(solution)/shard_map/store_results/pallas_call | solution.py:517
